TPU v7x, 128 devices: a whole 4x4x4 slice. The times are simulated.
128 devices in a mesh: gx: 8 (over y, core), gy: 16 (over z, x).
Axes of the slice: x: 4, y: 4, z: 4, core: 2. Of those that a mesh axis runs over, the one named last changes fastest.
Arguments:
- points: bfloat16 [131072, 64], P(('gx', 'gy')), may hold values from -25 to 25
- solution: float32 [131072, 32], P(('gx', 'gy')), may hold values from -6 to 6
- residual: float32 [131072, 32], P(('gx', 'gy')), may hold values from -36 to 36
- near_leaves: int32 [256, 4], P(('gx', 'gy')), may hold values from 0 to 255, as said below
- node_skeleton: int32 [128, 128], P(('gx', 'gy')), may hold values from 0 to 1023, as said below
- upper_skeleton: int32 [127, 128], replicated, may hold values from 0 to 255, as said below
- far_nodes: int32 [256, 16], P(('gx', 'gy')), may hold values from 0 to 254, as said below
Outputs:
- solution_next: float32 [131072, 32], P(('gx', 'gy'))
- residual_next: float32 [131072, 32], P(('gx', 'gy'))
- matvec_image: float32 [131072, 32], P(('gx', 'gy'))
Inputs may be any that keep to these rules, and one draw needn't show every extreme that they name: `near_leaves`: leaves are numbered in point order, 2 to a device in the flat device order. A leaf's 4 near leaves are distinct and lie on other devices of its gx row; the near leaves named by one device's leaves are all distinct, at most 1 of them lie on any one other device, and exactly 1 on some. `node_skeleton`: each row holds 128 distinct positions among its device's 1024 points. `upper_skeleton`: row u holds 128 distinct positions among the 256 skeleton points of nodes 2u+1 and 2u+2, those of 2u+1 first. `far_nodes`: each row holds 16 distinct tree nodes.
All inputs are finite; a program needn't handle non-finite values.
Results may differ from a plain program's by a relative error of at most 0.0033.
Values may be sent and summed in bfloat16 or wider, within the bound.
A program may use at most 128 MiB of HBM per device.

v0:
```python
import functools
import math

import jax
import jax.numpy as jnp
from jax import lax
from jax.sharding import Mesh
from jax.sharding import PartitionSpec as P

D = 64
NRHS = 32
LEAF = 512
RANK = 128
NEAR = 4
FAR = 16
LEAF_DEV = 2
GX = ("gx_0", "gx_1")
GY = ("gy_0", "gy_1")
GX_GY = ("gx_0", "gx_1", "gy_0", "gy_1")


LAMBDA_RIDGE = 1.0
FULL_PRECISION = lax.Precision.HIGHEST


def sent_together(arrays, axis, dim, along):
    ends, at = ([], 0)
    for a in arrays[:-1]:
        at += a.shape[along]
        ends.append(at)
    both = jnp.concatenate(arrays, axis=along)
    return tuple(jnp.split(lax.all_gather(both, axis, axis=dim, tiled=True), ends, axis=along))


def sent_to_all(shard, axis):
    copies = jnp.broadcast_to(shard, (lax.axis_size(axis), *shard.shape))
    return lax.all_to_all(copies, axis, split_axis=0, concat_axis=0, tiled=True)


def joined_along(pieces, dim):
    pieces = jnp.moveaxis(pieces, 0, dim)
    lengths = pieces.shape
    return pieces.reshape(*lengths[:dim], lengths[dim] * lengths[dim + 1], *lengths[dim + 2 :])


def collect(shard, axis, dim):
    pieces = sent_to_all(shard, axis)
    return joined_along(pieces, dim)


def cut_rows(length, count):
    step = length // count
    if step >= 8:
        step -= step % 8
    return [step * k for k in range(1, count)]


def stacked_from(shard, axes, turns):
    pieces = shard[None]
    for k in turns:
        pieces = lax.all_gather(pieces, axes[k], axis=0, tiled=True)
    current = [lax.axis_size(axes[k]) for k in reversed(turns)]
    pieces = pieces.reshape(*current, *shard.shape)
    turned = sorted(range(len(turns)), key=lambda place: turns[len(turns) - 1 - place])
    return pieces.transpose(*turned, *range(len(turns), pieces.ndim)).reshape(-1, *shard.shape)


def gather_at_once(shard, axes, dim):
    numbers = list(range(len(axes)))[::-1]
    widest = shard.shape.index(max(shard.shape[:-1] or shard.shape))
    edges = [0, *cut_rows(shard.shape[widest], len(axes)), shard.shape[widest]]
    done = []
    for k, (start, end) in enumerate(zip(edges, edges[1:])):
        if end > start:
            section = lax.slice_in_dim(shard, start, end, axis=widest)
            done.append(stacked_from(section, axes, numbers[k:] + numbers[:k]))
    return joined_along(jnp.concatenate(done, axis=widest + 1), dim)


def over_axes(shard, axes):
    return functools.reduce(lax.psum, axes, shard)


def kernel_tile(left_points, right_points):
    left_square = jnp.sum(jnp.square(left_points.astype(jnp.float32)), axis=-1)
    right_square = jnp.sum(jnp.square(right_points.astype(jnp.float32)), axis=-1)
    cross_term = jnp.dot(left_points, right_points.T, preferred_element_type=jnp.float32)
    distance = left_square[:, None] + right_square[None, :] - 2.0 * cross_term
    return jnp.exp(distance * (-0.5 / left_points.shape[-1]))


def kernel_batch(left_points, right_points):
    left_wide = left_points.astype(jnp.float32)
    right_wide = right_points.astype(jnp.float32)
    left_square = jnp.sum(left_wide * left_wide, axis=-1)
    right_square = jnp.sum(right_wide * right_wide, axis=-1)
    cross_term = jnp.einsum("bmd,bnd->bmn", left_wide, right_wide, precision=FULL_PRECISION)
    distance = left_square[:, :, None] + right_square[:, None, :] - 2.0 * cross_term
    return jnp.exp(distance * (-0.5 / left_points.shape[-1]))


def far_kernel(own_points, far_points):
    own_square = jnp.sum(jnp.square(own_points.astype(jnp.float32)), axis=-1)
    far_square = jnp.sum(jnp.square(far_points.astype(jnp.float32)), axis=-1)
    cross_term = jnp.einsum(
        "id,frd->fir", own_points, far_points, preferred_element_type=jnp.float32
    )
    distance = own_square[None, :, None] + far_square[:, None, :] - 2.0 * cross_term
    return jnp.exp(distance * (-0.5 / own_points.shape[-1]))


def cholesky_solve(matrix, right_side):
    order = matrix.shape[0]
    indices = jnp.arange(order, dtype=jnp.int32)

    def unit(column):
        return (indices == column).astype(matrix.dtype)

    def factor_step(column, lower):
        pick = unit(column)
        matrix_column = jnp.dot(matrix, pick, precision=FULL_PRECISION)
        lower_row = jnp.dot(pick, lower, precision=FULL_PRECISION)
        remainder = matrix_column - jnp.dot(lower, lower_row, precision=FULL_PRECISION)
        pivot = jnp.sqrt(jnp.sum(remainder * pick))
        new_column = jnp.where(indices >= column, remainder / pivot, jnp.zeros_like(remainder))
        return lower + new_column[:, None] * pick[None, :]

    lower = lax.fori_loop(0, order, factor_step, jnp.zeros_like(matrix))
    diagonal_part = jnp.sum(lower * jnp.eye(order, dtype=matrix.dtype), axis=1)

    def forward_step(column, partial_value):
        pick = unit(column)
        lower_row = jnp.dot(pick, lower, precision=FULL_PRECISION)
        value = (
            jnp.dot(pick, right_side, precision=FULL_PRECISION)
            - jnp.dot(lower_row, partial_value, precision=FULL_PRECISION)
        ) / jnp.sum(diagonal_part * pick)
        return partial_value + pick[:, None] * value[None, :]

    half_solve = lax.fori_loop(0, order, forward_step, jnp.zeros_like(right_side))

    def backward_step(count, partial_value):
        column = order - 1 - count
        pick = unit(column)
        lower_column = jnp.dot(lower, pick, precision=FULL_PRECISION)
        value = (
            jnp.dot(pick, half_solve, precision=FULL_PRECISION)
            - jnp.dot(lower_column, partial_value, precision=FULL_PRECISION)
        ) / jnp.sum(diagonal_part * pick)
        return partial_value + pick[:, None] * value[None, :]

    return lax.fori_loop(0, order, backward_step, jnp.zeros_like(right_side))


def build_levels(level_points, level_weights, upper_skeleton, level_top, level_stop, block_index):
    point_levels = [level_points]
    weight_levels = [level_weights]
    for level_now in range(level_top - 1, level_stop - 1, -1):
        half_count = level_points.shape[0] // 2
        child_points = level_points.reshape(
            half_count, 2 * level_points.shape[1], level_points.shape[2]
        )
        child_weights = level_weights.reshape(
            half_count, 2 * level_weights.shape[1], level_weights.shape[2]
        )
        pick_rows = lax.dynamic_slice_in_dim(
            upper_skeleton, 2**level_now - 1 + block_index * half_count, half_count, 0
        )
        level_points = jax.vmap(
            lambda group_points, group_picks: jnp.take(group_points, group_picks, axis=0)
        )(child_points, pick_rows)
        transfer = kernel_batch(level_points, child_points)
        level_weights = (
            jnp.einsum("bmn,bnc->bmc", transfer, child_weights, precision=FULL_PRECISION)
            / jnp.sum(transfer, axis=2)[:, :, None]
        )
        point_levels.insert(0, level_points)
        weight_levels.insert(0, level_weights)
    return (point_levels, weight_levels)


def split_levels(gathered, group_total):
    per_group = gathered.reshape(group_total, -1, gathered.shape[1], gathered.shape[2])
    pieces_out = []
    width_now = 1
    offset = 0
    while offset < per_group.shape[1]:
        pieces_out.append(
            per_group[:, offset : offset + width_now].reshape(
                group_total * width_now, gathered.shape[1], gathered.shape[2]
            )
        )
        offset = offset + width_now
        width_now = width_now * 2
    return pieces_out


def leaf_image(inputs):
    own_points, near_points, near_values, far_points, far_weights = inputs
    near_tiles = jax.vmap(lambda other_points: kernel_tile(own_points, other_points))(
        near_points
    ).astype(jnp.bfloat16)
    near_part = jnp.einsum(
        "nij,njc->ic", near_tiles, near_values, preferred_element_type=jnp.float32
    )
    far_tiles = far_kernel(own_points, far_points)
    far_part = jnp.einsum("fir,frc->ic", far_tiles, far_weights, precision=FULL_PRECISION)
    return near_part / math.sqrt(own_points.shape[0]) + far_part / far_points.shape[1]


def shards(points, solution, residual, near_leaves, node_skeleton, upper_skeleton, far_nodes):
    gx_count = lax.axis_size(GX)
    gy_count = lax.axis_size(GY)
    row_index = lax.axis_index(GX)
    values_half = residual.astype(jnp.bfloat16)
    flat_points = points.reshape(LEAF_DEV, LEAF * D)
    flat_values = values_half.reshape(LEAF_DEV, LEAF * NRHS)
    request_total = LEAF_DEV * NEAR
    wanted_leaves = near_leaves.reshape(request_total) - row_index * (gy_count * LEAF_DEV)
    piece_points, piece_values = sent_together((flat_points, flat_values), GY, 0, 1)
    positions = jnp.arange(piece_points.shape[0], dtype=jnp.int32)
    onehot = (wanted_leaves[:, None] == positions[None, :]).astype(jnp.bfloat16)
    got_points = jnp.dot(onehot, piece_points, preferred_element_type=jnp.float32)
    got_values = jnp.dot(onehot, piece_values, preferred_element_type=jnp.float32)
    fetched_points = got_points.astype(jnp.bfloat16)
    fetched_values = got_values.astype(jnp.bfloat16)
    own_points = points.reshape(LEAF_DEV, LEAF, D)
    near_points = jnp.concatenate(
        [own_points[:, None], fetched_points.reshape(LEAF_DEV, NEAR, LEAF, D)], axis=1
    )
    near_values = jnp.concatenate(
        [
            values_half.reshape(LEAF_DEV, 1, LEAF, NRHS),
            fetched_values.reshape(LEAF_DEV, NEAR, LEAF, NRHS),
        ],
        axis=1,
    )
    skeleton_points = jnp.take(points, node_skeleton[0], axis=0)
    node_weights = jnp.dot(
        kernel_tile(skeleton_points, points), residual, precision=FULL_PRECISION
    ) / math.sqrt(points.shape[0])
    depth_total = (gx_count * gy_count).bit_length() - 1
    row_depth = gx_count.bit_length() - 1
    row_points = collect(skeleton_points[None], GY, 0)
    row_weights = collect(node_weights[None], GY, 0)
    lower_points, lower_weights = build_levels(
        row_points, row_weights, upper_skeleton, depth_total, row_depth, row_index
    )
    every_points = lax.all_gather(jnp.concatenate(lower_points, axis=0), GX, axis=0, tiled=True)
    every_weights = gather_at_once(
        jnp.concatenate(lower_weights, axis=0).astype(jnp.bfloat16), GX, 0
    ).astype(jnp.float32)
    middle_points = split_levels(every_points, gx_count)
    middle_weights = split_levels(every_weights, gx_count)
    top_points, top_weights = build_levels(
        middle_points[0], middle_weights[0], upper_skeleton, row_depth, 0, 0
    )
    point_levels = top_points[:-1] + middle_points
    weight_levels = top_weights[:-1] + middle_weights
    tree_points = jnp.concatenate(point_levels, axis=0)
    tree_weights = jnp.concatenate(weight_levels, axis=0)
    far_flat = far_nodes.reshape(-1)
    far_points = jnp.take(tree_points, far_flat, axis=0).reshape(LEAF_DEV, FAR, RANK, D)
    far_weights = jnp.take(tree_weights, far_flat, axis=0).reshape(LEAF_DEV, FAR, RANK, NRHS)
    leaf_terms = lax.map(
        leaf_image, (own_points, near_points, near_values, far_points, far_weights)
    )
    matvec_image = LAMBDA_RIDGE * residual + leaf_terms.reshape(points.shape[0], NRHS)
    gram_matrix, cross_product = (
        over_axes(jnp.dot(matvec_image.T, matvec_image, precision=FULL_PRECISION), GX_GY),
        over_axes(jnp.dot(matvec_image.T, residual, precision=FULL_PRECISION), GX_GY),
    )
    step_coeffs = cholesky_solve(gram_matrix, cross_product)
    solution_next = solution + jnp.dot(residual, step_coeffs, precision=FULL_PRECISION)
    residual_next = residual - jnp.dot(matvec_image, step_coeffs, precision=FULL_PRECISION)
    return (solution_next, residual_next, matvec_image)


def solution(mesh):
    torus = Mesh(mesh.devices.reshape(4, 2, 4, 4), ("gx_0", "gx_1", "gy_0", "gy_1"))
    return jax.shard_map(
        shards,
        mesh=torus,
        in_specs=(
            P(GX_GY, None),
            P(GX_GY, None),
            P(GX_GY, None),
            P(GX_GY, None),
            P(GX_GY, None),
            P(),
            P(GX_GY, None),
        ),
        out_specs=(P(GX_GY, None), P(GX_GY, None), P(GX_GY, None)),
        check_vma=False,
    )
```

profile of v0, /device:TPU:1, one launch (start us, length us, event | category | flops | bytes accessed | tf_op | source)
XLA Modules:
  0.0 429.8 jit_solution(709872016097978637)
XLA Ops:
  14.6 8.4 %all-to-all-start = ((bf16[16,1,128,64]{2,3,1,0:T(8,128)(2,1)}), bf16[16,1,128,64]{2,3,1,0:T(8,128)(2,1)S(1)}, u32[]{:S(2)}, u32[]{:S(2)}) async-start(bf16[16,1,128,64]{2,3,1,0:T(8,128)(2,1)} %broadcast_in_dim.149), calls=%async_computation | async-start | bytes 524288 | tf_op jit(solution)/shard_map/all_to_all | solution.py:37
  31.0 5.8 %gather_fusion.3 = bf16[1024,64]{1,0:T(8,128)(2,1)S(1)} fusion(bf16[8,256,64]{2,1,0:T(8,128)(2,1)S(1)} %bitcast.407, s32[1024]{0:T(1024)S(1)} %fusion.159), kind=kCustom, calls=%fused_computation.9 | custom fusion | bytes 270336 | tf_op jit(solution)/shard_map/vmap(jit(_take))/gather | solution.py:170
  37.1 3.2 gather_fusion.4
  47.6 5.2 %all-to-all-start.1 = ((f32[16,1,128,32]{2,3,1,0:T(8,128)}), f32[16,1,128,32]{2,3,1,0:T(8,128)S(1)}, u32[]{:S(2)}, u32[]{:S(2)}) async-start(f32[16,1,128,32]{2,3,1,0:T(8,128)} %broadcast_in_dim.156), calls=%async_computation.1 | async-start | bytes 524288 | tf_op jit(solution)/shard_map/all_to_all | solution.py:37
  54.5 9.4 %all-to-all-done.1 = f32[16,1,128,32]{2,3,1,0:T(8,128)S(1)} async-done(((f32[16,1,128,32]{2,3,1,0:T(8,128)}), f32[16,1,128,32]{2,3,1,0:T(8,128)S(1)}, u32[]{:S(2)}, u32[]{:S(2)}) %all-to-all-start.1) | async-done | bytes 262176 | tf_op jit(solution)/shard_map/all_to_all | solution.py:37
  70.2 4.5 %all-gather = bf16[62,64,32]{1,2,0:T(8,128)(2,1)S(1)} all-gather(bf16[31,64,32]{1,2,0:T(8,128)(2,1)S(1)} %get-tuple-element.508), channel_id=2, replica_groups=mesh['gx_0'=4,'gx_1'=2,'gy_0'=4,'gy_1'=4] {'gx_1'}, dimensions={0}, use_global_device_ids=true | all-gather | bytes 380928 | tf_op jit(solution)/shard_map/all_gather | solution.py:61
  74.7 20.2 %all-gather.1 = bf16[124,64,32]{1,2,0:T(8,128)(2,1)S(1)} all-gather(bf16[31,64,32]{1,2,0:T(8,128)(2,1)S(1)} %get-tuple-element.507), channel_id=3, replica_groups=mesh['gx_0'=4,'gx_1'=2,'gy_0'=4,'gy_1'=4] {'gx_0'}, dimensions={0}, use_global_device_ids=true | all-gather | bytes 634880 | tf_op jit(solution)/shard_map/all_gather | solution.py:61
  95.0 4.8 %all_gather.23 = bf16[8,31,64,32]{2,3,1,0:T(8,128)(2,1)S(1)} all-gather(bf16[4,31,64,32]{2,3,1,0:T(8,128)(2,1)S(1)} %bitcast.427), channel_id=1, replica_groups=mesh['gx_0'=4,'gx_1'=2,'gy_0'=4,'gy_1'=4] {'gx_1'}, dimensions={0}, use_global_device_ids=true | all-gather | bytes 1523712 | tf_op jit(solution)/shard_map/all_gather | solution.py:61
  100.4 20.2 %all_gather.21 = bf16[8,31,64,32]{2,3,0,1:T(8,128)(2,1)S(1)} all-gather(bf16[2,31,64,32]{2,3,0,1:T(8,128)(2,1)S(1)} %copy.233), channel_id=1, replica_groups=mesh['gx_0'=4,'gx_1'=2,'gy_0'=4,'gy_1'=4] {'gx_0'}, dimensions={0}, use_global_device_ids=true | all-gather | bytes 1269760 | tf_op jit(solution)/shard_map/all_gather | solution.py:61
  132.4 3.3 reshape.524
  136.9 3.0 reshape.392
  153.0 3.1 slice.79
  157.3 3.2 gather_fusion.7
  175.6 3.2 constant_dynamic-update-slice_fusion.3
  191.1 15.8 %while.53 = (s32[]{:T(128)}, f32[2,512,32]{1,0,2:T(2,128)}, bf16[2,512,64]{1,2,0:T(8,128)(2,1)S(1)}, bf16[2,5,512,64]{2,3,1,0:T(8,128)(2,1)S(1)}, bf16[2,5,512,3...) while((s32[]{:T(128)}, f32[2,512,32]{1,0,2:T(2,128)}, ...), condition=%wide.region_22.26_spmd, body=%wide.region_18.25_spmd.sunk | while | flops 800304128 | bytes 11750065 | solution.py:265
  192.2 3.5 fusion.265
  199.9 3.5 fusion.265
  208.3 13.3 %all-reduce.2 = (f32[32,32]{1,0:T(8,128)S(1)}, f32[32,32]{1,0:T(8,128)S(1)}) all-reduce(f32[32,32]{1,0:T(8,128)S(1)} %fusion.178, f32[32,32]{1,0:T(8,128)S(1)} %fusion.179), channel_id=1, replica_groups=mesh['gx_0'=4,'gx_1'=2,'gy_0'=4,'gy_1'=4] {'gx_0'}, use_global_device_ids=true, to_apply=%region_30.34 | all-reduce | flops 2048 | bytes 16384 | tf_op jit(solution)/shard_map/psum | solution.py:81
  221.6 8.2 %all-reduce.3 = (f32[32,32]{1,0:T(8,128)S(1)}, f32[32,32]{1,0:T(8,128)S(1)}) all-reduce(f32[32,32]{1,0:T(8,128)S(1)} %get-tuple-element.485, f32[32,32]{1,0:T(8,128)S(1)} %get-tuple-element.486), channel_id=1, replica_groups=mesh['gx_0'=4,'gx_1'=2,'gy_0'=4,'gy_1'=4] {'gx_1'}, use_global_device_ids=true, to_apply=%region_31.35 | all-reduce | flops 2048 | bytes 16384 | tf_op jit(solution)/shard_map/psum | solution.py:81
  229.8 11.3 %all-reduce.1 = (f32[32,32]{1,0:T(8,128)S(1)}, f32[32,32]{1,0:T(8,128)S(1)}) all-reduce(f32[32,32]{1,0:T(8,128)S(1)} %get-tuple-element.487, f32[32,32]{1,0:T(8,128)S(1)} %get-tuple-element.488), channel_id=1, replica_groups=mesh['gx_0'=4,'gx_1'=2,'gy_0'=4,'gy_1'=4] {'gy_0'}, use_global_device_ids=true, to_apply=%region_32.36 | all-reduce | flops 2048 | bytes 16384 | tf_op jit(solution)/shard_map/psum | solution.py:81
  241.1 11.0 %all-reduce = (f32[32,32]{1,0:T(8,128)S(1)}, f32[32,32]{1,0:T(8,128)S(1)}) all-reduce(f32[32,32]{1,0:T(8,128)S(1)} %get-tuple-element.483, f32[32,32]{1,0:T(8,128)S(1)} %get-tuple-element.484), channel_id=1, replica_groups=mesh['gx_0'=4,'gx_1'=2,'gy_0'=4,'gy_1'=4] {'gy_1'}, use_global_device_ids=true, to_apply=%region_33.37 | all-reduce | flops 2048 | bytes 16384 | tf_op jit(solution)/shard_map/psum | solution.py:81
  252.1 57.9 %while.56 = (s32[]{:T(128)}, f32[32,32]{1,0:T(8,128)S(1)}, f32[32,32]{1,0:T(8,128)S(1)}, s32[]{:T(128)}, s32[]{:T(128)}) while((s32[]{:T(128)}, f32[32,32]{1,0:T(8,128)S(1)}, f32[32,32]{1,0:T(8,128)S(1)}, s32[]{:T(128)}, s32[]{:T(128)}) %tuple.141), condition=%wide.region_29.33_spmd.clone.clone, body=%wide.region_27.32_spmd.clone.clone.sunk | while | flops 42338 | bytes 21877 | solution.py:128
  310.1 55.3 %while.54 = (s32[]{:T(128)}, f32[32,32]{1,0:T(8,128)S(1)}, f32[32,32]{1,0:T(8,128)S(1)}, f32[32,32]{1,0:T(8,128)S(1)}, f32[32]{0:T(128)S(1)}, /*index=5*/s32[]{:T(128)}, s32[]{:T(128)}) while((s32[]{:T(128)}, f32[32,32]{1,0:T(8,128)S(1)}, f32[32,32]{1,0:T(8,128)S(1)}, f32[32,32]{1,0:T(8,128)S(1)}, f32[32]{0:T(128)S(1)}, ...), condition=%wide.region_37.41_spmd.clone, body=%wide.region_35.40_spmd.clone.sunk | while | flops 41250 | bytes 21752 | solution.py:140
  365.4 55.6 %while.55 = (s32[]{:T(128)}, f32[32,32]{1,0:T(8,128)S(1)}, f32[32,32]{1,0:T(8,128)S(1)}, f32[32,32]{1,0:T(8,128)S(1)}, f32[32]{0:T(128)S(1)}, /*index=5*/s32[]{:T(128)}, s32[]{:T(128)}, s32[]{:T(128)}) while((s32[]{:T(128)}, f32[32,32]{1,0:T(8,128)S(1)}, f32[32,32]{1,0:T(8,128)S(1)}, f32[32,32]{1,0:T(8,128)S(1)}, ...), condition=%wide.region_40.44_spmd.clone, body=%wide.region_38.43_spmd.clone.sunk | while | flops 41251 | bytes 21772 | solution.py:152
  (798 shorter events, 243.5 us)
Async XLA Ops:
  7.2 125.3 %all-gather.8.cloned.1.call-start = ((), (), s32[]{:S(2)}) async-start(), calls=%async_computation.3 | async-start | bytes 3342336 | tf_op jit(solution)/shard_map/all_gather | solution.py:32
  9.7 14.6 %copy-start.4 = (bf16[1024,64]{1,0:T(8,128)(2,1)}, bf16[1024,64]{1,0:T(8,128)(2,1)S(1)}, u32[]{:S(2)}) copy-start(bf16[1024,64]{1,0:T(8,128)(2,1)S(1)} %copy.197) | copy-start | bytes 393220
  14.6 16.0 %all-to-all-start = ((bf16[16,1,128,64]{2,3,1,0:T(8,128)(2,1)}), bf16[16,1,128,64]{2,3,1,0:T(8,128)(2,1)S(1)}, u32[]{:S(2)}, u32[]{:S(2)}) async-start(bf16[16,1,128,64]{2,3,1,0:T(8,128)(2,1)} %broadcast_in_dim.149), calls=%async_computation | async-start | bytes 524288 | tf_op jit(solution)/shard_map/all_to_all | solution.py:37
  23.1 125.6 %all-gather.6.cloned.1.call-start = ((), (), s32[]{:S(2)}) async-start(), calls=%async_computation.2 | async-start | bytes 4571136 | tf_op jit(solution)/shard_map/all_gather | solution.py:249
  31.0 15.0 %copy-start.7 = (bf16[1024,64]{0,1:T(8,128)(2,1)S(1)}, bf16[1024,64]{0,1:T(8,128)(2,1)}, u32[]{:S(2)}) copy-start(bf16[1024,64]{0,1:T(8,128)(2,1)} %param.21) | copy-start | bytes 393220
  31.0 15.3 %copy-start.3 = (f32[1024,32]{0,1:T(8,128)S(1)}, f32[1024,32]{0,1:T(8,128)}, u32[]{:S(2)}) copy-start(f32[1024,32]{0,1:T(8,128)} %param.23) | copy-start | bytes 393220
  37.0 15.9 %copy-start.18 = (s32[2,4]{1,0:T(2,128)S(1)}, s32[2,4]{1,0:T(2,128)}, u32[]{:S(2)}) copy-start(s32[2,4]{1,0:T(2,128)} %param.24) | copy-start | bytes 100
  37.0 16.6 %copy-start.19 = (s32[2,16]{1,0:T(2,128)S(1)}, s32[2,16]{1,0:T(2,128)}, u32[]{:S(2)}) copy-start(s32[2,16]{1,0:T(2,128)} %param.27) | copy-start | bytes 388
  44.7 8.2 %copy-start.14 = (bf16[1,128,64]{2,1,0:T(8,128)(2,1)}, bf16[1,128,64]{2,1,0:T(8,128)(2,1)S(1)}, u32[]{:S(2)}) copy-start(bf16[1,128,64]{2,1,0:T(8,128)(2,1)S(1)} %get-tuple-element.494) | copy-start | bytes 49156
  47.6 16.3 %all-to-all-start.1 = ((f32[16,1,128,32]{2,3,1,0:T(8,128)}), f32[16,1,128,32]{2,3,1,0:T(8,128)S(1)}, u32[]{:S(2)}, u32[]{:S(2)}) async-start(f32[16,1,128,32]{2,3,1,0:T(8,128)} %broadcast_in_dim.156), calls=%async_computation.1 | async-start | bytes 524288 | tf_op jit(solution)/shard_map/all_to_all | solution.py:37
  121.6 2.3 copy-start
  124.6 6.3 %slice-start = ((f32[8,31,128,32]{2,3,0,1:T(8,128)}), f32[8,16,128,32]{2,3,0,1:T(8,128)S(1)}, s32[]{:S(2)}) async-start(f32[8,31,128,32]{2,3,0,1:T(8,128)} %copy-done), calls=%async_computation.4 | async-start | bytes 4194304 | tf_op jit(solution)/shard_map/slice | solution.py:189
  132.4 3.3 copy-start.17
  151.7 8.9 %copy-start.16 = (pred[4,128]{1,0:T(4,128)(4,1)S(1)}, pred[4,128]{1,0:T(4,128)(4,1)}, u32[]{:S(2)}) copy-start(pred[4,128]{1,0:T(4,128)(4,1)} %get-tuple-element.514) | copy-start | bytes 1540
  153.0 10.6 %copy-start.15 = (pred[128]{0:T(512)(128)(4,1)S(1)}, pred[128]{0:T(512)(128)(4,1)}, u32[]{:S(2)}) copy-start(pred[128]{0:T(512)(128)(4,1)} %get-tuple-element.509) | copy-start | bytes 388
  153.0 14.7 %copy-start.10 = (bf16[4,256,32]{1,0,2:T(4,128)(2,1)S(1)}, bf16[4,256,32]{1,0,2:T(4,128)(2,1)}, u32[]{:S(2)}) copy-start(bf16[4,256,32]{1,0,2:T(4,128)(2,1)} %reshape_reshape.15) | copy-start | bytes 196612
  174.5 8.8 %copy-start.6 = (f32[8,4,128,32]{2,3,1,0:T(8,128)S(1)}, f32[8,4,128,32]{2,3,1,0:T(8,128)}, u32[]{:S(2)}) copy-start(f32[8,4,128,32]{2,3,1,0:T(8,128)} %copy.241) | copy-start | bytes 1572868
  175.6 10.9 %copy-start.1 = (f32[8,16,128,32]{2,3,1,0:T(8,128)S(1)}, f32[8,16,128,32]{2,3,1,0:T(8,128)}, u32[]{:S(2)}) copy-start(f32[8,16,128,32]{2,3,1,0:T(8,128)} %copy.243) | copy-start | bytes 6291460
  187.9 3.1 copy-start.2
  187.9 3.1 copy-start.9
  191.0 230.9 %copy-start.11 = (f32[1024,32]{0,1:T(8,128)S(1)}, f32[1024,32]{0,1:T(8,128)}, u32[]{:S(2)}) copy-start(f32[1024,32]{0,1:T(8,128)} %param.22) | copy-start | bytes 393220
  195.7 2.1 copy-start.12
  203.5 2.1 copy-start.12
  207.8 215.1 %copy-start.5 = (f32[1024,32]{0,1:T(8,128)}, f32[1024,32]{0,1:T(8,128)S(1)}, u32[]{:S(2)}) copy-start(f32[1024,32]{0,1:T(8,128)S(1)} %add.389) | copy-start | bytes 393220
  (3 other events, 2.1 us)
Sparse Core Ops, SparseCore 0:
  10.9 55.3 all-gather.7
  68.0 38.0 all-gather.5
where the time goes:
time: 438 us; the launch traced here: 430 us
  matrix products  124 us (28%)
  blocking collectives  93.4 us (21%)
  local copies, waits for them, and re-layouts  83.5 us (19%)
  other arithmetic  66.1 us (15%)
  loops' own time  23.1 us (5%)
  between operations  14.9 us (3%)
  starting transfers between devices  13.8 us (3%)
  waiting for transfers between devices  10.9 us (2%)
    all_gather x4, blocking collectives, stacked_from(): pieces = lax.all_gather(pieces, axes[k], axis=0, tiled=True)  49.7 us
    psum x4, blocking collectives, over_axes(): return functools.reduce(lax.psum, axes, shard)  43.8 us
    dot_general x32, matrix products, forward_step(): jnp.dot(lower_row, partial_value, precision=FULL_PRECISION)  24.7 us
    dot_general x32, matrix products, backward_step(): jnp.dot(lower_column, partial_value, precision=FULL_PRECISION)  24.7 us
    dot_general x32, matrix products, factor_step(): jnp.dot(lower, lower_row, precision=FULL_PRECISION)  24.5 us
    another operation x1, loops' own time, cholesky_solve(): lower = lax.fori_loop(0, order, factor_step, jnp.zeros_like(matrix))  22.5 us
    reduce_sum x32, other arithmetic, backward_step(): jnp.sum(diagonal_part * pick)  20.2 us
    unnamed x55, local copies, waits for them, and re-layouts  19.9 us
  transfers between devices with their start and end apart: 4, of which 2 were waited for; matrix products, arithmetic and copies ran while one was open for 14% of the time, Pallas kernels for 0%

commit v1 on v0

v1 whole, which is shorter than its diff:
```python
import math

import jax
import jax.numpy as jnp
from jax import lax
from jax.experimental import pallas as pl
from jax.experimental.pallas import tpu as pltpu
from jax.sharding import PartitionSpec as P

D = 64
NRHS = 32
LEAF = 512
RANK = 128
NEAR = 4
FAR = 16
CPD = 1024
N_GX = 8
N_GY = 16
N_Y = 4
NODES = 255
FIRST = 127
AUG = D + 16
PAY = AUG + NRHS
REQ = PAY + 16
LEAF_ROWS = D + NRHS
SCALE = math.log2(math.e) / D
FULL = lax.Precision.HIGHEST
F32, BF16 = jnp.float32, jnp.bfloat16
MESH = pl.DeviceIdType.MESH


def dot(a, b, contract=((1,), (0,)), precision=None):
    return lax.dot_general(a, b, (contract, ((), ())), precision=precision, preferred_element_type=F32)


def square_rows(wide):
    half = -0.5 * jnp.sum(wide * wide, axis=0, keepdims=True)
    high = half.astype(BF16).astype(F32)
    rest = half - high
    middle = rest.astype(BF16).astype(F32)
    low = rest - middle
    row = lax.broadcasted_iota(jnp.int32, (16, wide.shape[1]), 0)
    ones = jnp.where((row >= 4) & (row < 7), 1.0, 0.0)
    return jnp.where(row == 0, high, jnp.where(row == 1, middle, jnp.where(row == 2, low, ones)))


def turned(rows):
    return jnp.concatenate([pltpu.roll(rows[:8], 4, 0), rows[8:]], axis=0)


def kernel_body(
    points, residual, near, requests, skeleton, upper, far,
    image, coeffs,
    nodes, own, own_right, own_left, stage, near_in, near_acc, far_acc, part1, part2,
    pay_s, pay_r, near_s, near_r, y_s, y_r, sib_s, sib_r, one_s, one_r, two_s, two_r,
):
    gx, gy = lax.axis_index("gx"), lax.axis_index("gy")
    y, core = gx // 2, gx % 2
    me = gx * N_GY + gy
    sibling = 2 * y + (1 - core)

    barrier = pltpu.get_barrier_semaphore()

    @pl.loop(1, N_GY)
    def _(k):
        pl.semaphore_signal(barrier, inc=1, device_id=(gx, (gy + k) % N_GY), device_id_type=MESH)

    @pl.loop(1, N_GX)
    def _(k):
        pl.semaphore_signal(barrier, inc=1, device_id=((gx + k) % N_GX, gy), device_id_type=MESH)

    for leaf in range(2):
        at = pl.ds(leaf * LEAF, LEAF)
        wide = points[:, at].astype(F32)
        rows = square_rows(wide)
        own_right[leaf, 0:D] = points[:, at]
        own_right[leaf, D:AUG] = rows.astype(BF16)
        both = jnp.concatenate([wide, turned(rows), jnp.zeros((48, LEAF), F32)], axis=0)
        own_left[leaf] = both.T.astype(BF16)
        own[leaf, 0:D] = points[:, at]
        own[leaf, D:LEAF_ROWS] = residual[:, at].astype(BF16)
    pick = skeleton[...]
    skel = jnp.zeros((D, RANK), F32)
    for leaf in range(2):
        place = lax.broadcasted_iota(jnp.int32, (LEAF, RANK), 0) + leaf * LEAF
        skel += dot(points[:, pl.ds(leaf * LEAF, LEAF)], jnp.where(place == pick, 1.0, 0.0).astype(BF16))
    rows = square_rows(skel)
    left = jnp.concatenate([skel, turned(rows), jnp.zeros((48, RANK), F32)], axis=0).T.astype(BF16)
    weights = jnp.zeros((NRHS, RANK), F32)
    for leaf in range(2):
        tile = jnp.exp2(SCALE * dot(left[:, :AUG], own_right[leaf]))
        weights += dot(residual[:, pl.ds(leaf * LEAF, LEAF)], tile, ((1,), (1,)), FULL)
    mine = FIRST + me
    nodes[mine, 0:D] = skel.astype(BF16)
    nodes[mine, D:AUG] = rows.astype(BF16)
    nodes[mine, AUG:PAY] = (weights * (1.0 / math.sqrt(CPD))).astype(BF16)
    nodes[mine, PAY:REQ] = requests[...]

    pl.semaphore_wait(barrier, N_GY - 1 + N_GX - 1)

    def pay_copy(k, slot):
        peer = (gy + k) % N_GY
        return pltpu.make_async_remote_copy(
            src_ref=nodes.at[mine], dst_ref=nodes.at[slot],
            send_sem=pay_s.at[peer], recv_sem=pay_r.at[slot - FIRST - gx * N_GY],
            device_id=(gx, peer), device_id_type=MESH,
        )

    @pl.loop(1, N_GY)
    def _(k):
        pay_copy(k, mine).start()

    def tiles(leaf, right, values, acc, first):
        for c in range(4):
            at = pl.ds(c * 128, 128)
            tile = jnp.exp2(SCALE * dot(own_left[leaf, at, :AUG], right)).astype(BF16)
            term = dot(values, tile, ((1,), (1,)))
            acc[leaf, :, at] = term if first else acc[leaf, :, at] + term

    for leaf in range(2):
        tiles(leaf, own_right[leaf], own[leaf, D:LEAF_ROWS], near_acc, True)

    asked = (2 * me + 1).astype(F32)
    near_in[gy] = own[0]

    def near_copy(peer, slot):
        return pltpu.make_async_remote_copy(
            src_ref=stage.at[peer], dst_ref=near_in.at[slot],
            send_sem=near_s.at[peer], recv_sem=near_r.at[slot],
            device_id=(gx, peer), device_id_type=MESH,
        )

    @pl.loop(1, N_GY)
    def _(k):
        peer = (gy + k) % N_GY
        slot = FIRST + gx * N_GY + peer
        pay_copy(k, slot).wait_recv()
        want = nodes[slot, PAY:REQ].astype(F32)
        second = jnp.max(jnp.where(want == asked, 1.0, 0.0), axis=0, keepdims=True)
        second = jnp.concatenate([second] * 4, axis=1)
        for r in range(0, LEAF_ROWS, 32):
            at = pl.ds(r, 32)
            pick_second = jnp.broadcast_to(second, (32, LEAF))
            stage[peer, at] = jnp.where(
                pick_second > 0.5, own[1, at].astype(F32), own[0, at].astype(F32)
            ).astype(BF16)
        near_copy(peer, gy).start()

    def block(row):
        return nodes.at[pl.ds(FIRST + row * N_GY, N_GY), pl.ds(0, PAY)]

    def y_copy(k, row):
        other = (y + k) % N_Y
        return pltpu.make_async_remote_copy(
            src_ref=block(gx), dst_ref=block(row),
            send_sem=y_s.at[other], recv_sem=y_r.at[row // 2],
            device_id=(2 * other + core, gy), device_id_type=MESH,
        )

    def sib_copy(other, row):
        return pltpu.make_async_remote_copy(
            src_ref=block(2 * other + core), dst_ref=block(row),
            send_sem=sib_s.at[other], recv_sem=sib_r.at[row // 2],
            device_id=(sibling, gy), device_id_type=MESH,
        )

    for k in (1, 3, 2):
        y_copy(k, gx).start()
    sib_copy(y, gx).start()

    place = lax.broadcasted_iota(jnp.int32, (2 * RANK, RANK), 0)

    def build(first, count):
        done = []
        for i in range(count):
            u = first + i
            a, b = nodes[2 * u + 1, 0:PAY], nodes[2 * u + 2, 0:PAY]
            choice = jnp.where(place == upper[pl.ds(u, 1), :], 1.0, 0.0).astype(BF16)
            right = dot(jnp.concatenate([a[:AUG], b[:AUG]], axis=1), choice)
            left = jnp.concatenate([right[:D], turned(right[D:])], axis=0).astype(BF16)
            both = jnp.concatenate([a[:AUG], b[:AUG]], axis=1)
            tile = jnp.exp2(SCALE * dot(both, left, ((0,), (0,)))).astype(BF16)
            sums = dot(jnp.concatenate([a[D:], b[D:]], axis=1), tile)
            done.append((right.astype(BF16), (sums[16:] / sums[4:5]).astype(BF16)))
        for i, (right, weights) in enumerate(done):
            nodes[first + i, 0:AUG] = right
            nodes[first + i, AUG:PAY] = weights

    def build_row(row):
        build(63 + row * 8, 4)
        build(67 + row * 8, 4)
        build(31 + row * 4, 4)
        build(15 + row * 2, 2)
        build(7 + row, 1)

    build_row(gx)
    sib_copy(y, sibling).wait_recv()
    build_row(sibling)

    @pl.loop(1, N_Y)
    def _(k):
        other = (y + k) % N_Y
        y_copy(k, 2 * other + core).wait_recv()
        sib_copy(other, 2 * other + core).start()
        build_row(2 * other + core)

    @pl.loop(1, N_GY)
    def _(k):
        peer = (gy + k) % N_GY
        near_copy(peer, peer).wait_recv()

    for leaf in range(2):

        @pl.loop(0, NEAR)
        def _(n, leaf=leaf):
            got = near_in[(near[leaf, n] // 2) % N_GY]
            right = jnp.concatenate([got[:D], square_rows(got[:D].astype(F32)).astype(BF16)], axis=0)
            tiles(leaf, right, got[D:], near_acc, False)

    @pl.loop(1, N_Y)
    def _(k):
        other = (y + k) % N_Y
        row = 2 * other + 1 - core
        sib_copy(other, row).wait_recv()
        build_row(row)

    build(3, 4)
    build(1, 2)
    build(0, 1)

    far_acc[...] = jnp.zeros_like(far_acc)
    for leaf in range(2):

        @pl.loop(0, FAR // 4)
        def _(n, leaf=leaf):
            got = jnp.concatenate([nodes[far[leaf, 4 * n + i], 0:PAY] for i in range(4)], axis=1)
            tiles(leaf, got[:AUG], got[AUG:], far_acc, False)

    for leaf in range(2):
        at = pl.ds(leaf * LEAF, LEAF)
        image[:, at] = (
            residual[:, at] + near_acc[leaf] * (1.0 / math.sqrt(LEAF)) + far_acc[leaf] * (1.0 / RANK)
        )

    both = jnp.concatenate([image[...], residual[...]], axis=0)
    gram = dot(image[...], both, ((1,), (1,)), FULL)
    part1[gy] = jnp.concatenate([gram[:16], gram[16:]], axis=1)

    def one_copy(peer, slot):
        return pltpu.make_async_remote_copy(
            src_ref=part1.at[gy], dst_ref=part1.at[slot],
            send_sem=one_s.at[peer], recv_sem=one_r.at[slot],
            device_id=(gx, peer), device_id_type=MESH,
        )

    def two_copy(peer, slot):
        return pltpu.make_async_remote_copy(
            src_ref=part2.at[gx], dst_ref=part2.at[slot],
            send_sem=two_s.at[peer], recv_sem=two_r.at[slot],
            device_id=(peer, gy), device_id_type=MESH,
        )

    @pl.loop(1, N_GY)
    def _(k):
        one_copy((gy + k) % N_GY, gy).start()

    @pl.loop(1, N_GY)
    def _(k):
        peer = (gy + k) % N_GY
        one_copy(peer, peer).wait_recv()

    total = part1[0]
    for k in range(1, N_GY):
        total += part1[k]
    part2[gx] = total

    @pl.loop(1, N_GX)
    def _(k):
        two_copy((gx + k) % N_GX, gx).start()

    @pl.loop(1, N_GX)
    def _(k):
        peer = (gx + k) % N_GX
        two_copy(peer, peer).wait_recv()

    total = part2[0]
    for k in range(1, N_GX):
        total += part2[k]

    work = jnp.concatenate([total, pltpu.roll(total, 64, 1)], axis=0)
    row = lax.broadcasted_iota(jnp.int32, (NRHS, 128), 0)
    for k in range(NRHS):
        pivot_row = work[k : k + 1] / work[k : k + 1, k : k + 1]
        work = jnp.where(row == k, pivot_row, work - work[:, k : k + 1] * pivot_row)
    coeffs[...] = work

    @pl.loop(1, N_GY)
    def _(k):
        peer = (gy + k) % N_GY
        pay_copy(k, mine).wait_send()
        near_copy(peer, gy).wait_send()
        one_copy(peer, gy).wait_send()

    @pl.loop(1, N_GX)
    def _(k):
        two_copy((gx + k) % N_GX, gx).wait_send()

    for k in (1, 3, 2):
        y_copy(k, gx).wait_send()

    @pl.loop(0, N_Y)
    def _(k):
        sib_copy((y + k) % N_Y, gx).wait_send()


def shards(points, solution, residual, near_leaves, node_skeleton, upper_skeleton, far_nodes):
    requests = jnp.concatenate([near_leaves.reshape(-1), jnp.full((8,), -1, jnp.int32)])
    requests = jnp.broadcast_to(requests.astype(BF16)[:, None], (16, 128))
    vmem, smem = (pl.BlockSpec(memory_space=m) for m in (pltpu.VMEM, pltpu.SMEM))
    dma = pltpu.SemaphoreType.DMA
    residual_t = residual.T
    image_t, work = pl.pallas_call(
        kernel_body,
        out_shape=(
            jax.ShapeDtypeStruct((NRHS, CPD), F32),
            jax.ShapeDtypeStruct((NRHS, 128), F32),
        ),
        in_specs=[vmem, vmem, smem, vmem, vmem, vmem, smem],
        out_specs=(vmem, vmem),
        scratch_shapes=[
            pltpu.VMEM((NODES, REQ, RANK), BF16),
            pltpu.VMEM((2, LEAF_ROWS, LEAF), BF16),
            pltpu.VMEM((2, AUG, LEAF), BF16),
            pltpu.VMEM((2, LEAF, 128), BF16),
            pltpu.VMEM((N_GY, LEAF_ROWS, LEAF), BF16),
            pltpu.VMEM((N_GY, LEAF_ROWS, LEAF), BF16),
            pltpu.VMEM((2, NRHS, LEAF), F32),
            pltpu.VMEM((2, NRHS, LEAF), F32),
            pltpu.VMEM((N_GY, 16, 128), F32),
            pltpu.VMEM((N_GX, 16, 128), F32),
            dma((N_GY,)), dma((N_GY,)), dma((N_GY,)), dma((N_GY,)),
            dma((N_Y,)), dma((N_Y,)), dma((N_Y,)), dma((N_Y,)),
            dma((N_GY,)), dma((N_GY,)), dma((N_GX,)), dma((N_GX,)),
        ],
        compiler_params=pltpu.CompilerParams(
            collective_id=0, has_side_effects=True, vmem_limit_bytes=48 * 2**20
        ),
    )(points.T, residual_t, near_leaves, requests, node_skeleton, upper_skeleton, far_nodes)
    step = work[:, NRHS : 2 * NRHS]
    solution_next = solution.T + dot(step, residual_t, ((0,), (0,)), FULL)
    residual_next = residual_t - dot(step, image_t, ((0,), (0,)), FULL)
    return solution_next.T, residual_next.T, image_t.T


def solution(mesh):
    split = P(("gx", "gy"), None)
    return jax.shard_map(
        shards,
        mesh=mesh,
        in_specs=(split, split, split, split, split, P(), split),
        out_specs=(split, split, split),
        check_vma=False,
    )
```

time: 438 us -> 95.5 us (0.22); the launches traced: 430 us -> 95.3 us
  matrix products: 124 us -> 2.08 us
  blocking collectives: 93.4 us -> 0 us
  Pallas kernels: 0 us -> 87.8 us
  local copies, waits for them, and re-layouts: 83.5 us -> 4.75 us
  other arithmetic: 66.1 us -> 0.01 us
  loops' own time: 23.1 us -> 0 us
  between operations: 14.9 us -> 0.66 us
  starting transfers between devices: 13.8 us -> 0 us
  waiting for transfers between devices: 10.9 us -> 0 us
    dot_general x316 -> x2, matrix products: 124 us -> 2.08 us  [dot(): lax.dot_general(a, b, (contract, ((), ())), precision=precision, preferre...]
    pallas_call x0 -> x1, Pallas kernels: none -> 87.8 us  [shards(): pl.pallas_call(kernel_body, out_shape=(jax.ShapeDtypeStruct((NRHS, CPD),...]
    all_gather x4 -> x0, blocking collectives: 49.7 us -> none  [stacked_from(): pieces = lax.all_gather(pieces, axes[k], axis=0, tiled=True)]
    psum x4 -> x0, blocking collectives: 43.8 us -> none  [over_axes(): return functools.reduce(lax.psum, axes, shard)]
    reduce_sum x82 -> x0, other arithmetic: 43.3 us -> none  [the longest x32 20.2 us: backward_step(): jnp.sum(diagonal_part * pick)]
    gather x17 -> x0, local copies, waits for them, and re-layouts: 24.4 us -> none  [the longest x14 18 us: build_levels(): jnp.take(group_points, group_picks, axis=0)]
    another operation x4 -> x0, loops' own time: 23.1 us -> none  [the longest x1 22.5 us: cholesky_solve(): lower = lax.fori_loop(0, order, factor_step, jnp.zeros_like(matrix))]
    slice x16 -> x0, local copies, waits for them, and re-layouts: 16.6 us -> none  [the longest x15 16.4 us: split_levels(): per_group[:, offset:offset + width_now]]
  transfers between devices with their start and end apart: 4 -> 0, of which waited for: 2 -> 0; matrix products, arithmetic and copies ran while one was open for 14% -> 0% of each run, Pallas kernels for 0% -> 0%
where the time goes in v1:
time: 95.5 us; the launch traced here: 95.3 us
  Pallas kernels  87.8 us (92%)
  local copies, waits for them, and re-layouts  4.75 us (5%)
  matrix products  2.08 us (2%)
    pallas_call x1, Pallas kernels, shards(): pl.pallas_call(kernel_body, out_shape=(jax.ShapeDtypeStruct((NRHS, CPD),...  87.8 us
    unnamed x15, local copies, waits for them, and re-layouts  4.59 us
    dot_general x2, matrix products, dot(): lax.dot_general(a, b, (contract, ((), ())), precision=precision, preferre...  2.08 us

profile of v1, /device:TPU:1, one launch (start us, length us, event | category | flops | bytes accessed | tf_op | source)
XLA Modules:
  0.0 95.3 jit_solution(956846866183124356)
XLA Ops:
  0.6 0.0 copy-start.3
  0.6 0.7 copy-done.3
  1.3 0.1 reshape.11
  1.4 0.0 copy-start.4
  1.4 0.0 copy-start.5
  1.4 0.1 broadcast_in_dim.2.requests
  1.5 0.6 copy-done.4
  2.1 0.0 copy-done.5
  2.1 0.0 copy-start
  2.1 0.9 copy-done
  3.0 0.0 copy-start.1
  3.0 0.9 copy-done.1
  3.9 0.0 copy-start.2
  3.9 0.8 copy-done.2
  4.7 87.8 %shard_map.94 = (f32[32,1024]{1,0:T(8,128)S(1)}, f32[32,128]{1,0:T(8,128)S(1)}) custom-call(bf16[64,1024]{1,0:T(8,128)(2,1)S(1)} %bitcast.11, f32[32,1024]{1,0:T(8,128)S(1)} %bitcast.9, s32[2,4]{1,0:T(2,128)S(1)} %copy-done.3, bf16[16,128]{1,0:T(8,128)(2,1)S(1)} %broadcast_in_dim.2.requests, s32[1,128]{1,0:T(1,128)S(1)} %copy-done.5, ...), custom_call_target="tpu_custom_call" | custom-call | tf_op jit(solution)/shard_map/pallas_call | solution.py:322
  92.5 0.0 copy-start.6
  92.5 1.0 %convolution_subtract_fusion = f32[1024,32]{0,1:T(8,128)} fusion(f32[1024,32]{0,1:T(8,128)S(1)} %copy-done, f32[32,1024]{1,0:T(8,128)S(1)} %get-tuple-element.6, f32[32,128]{1,0:T(8,128)S(1)} %get-tuple-element.5), kind=kOutput, calls=%fused_computation | convolution fusion | flops 12615680 | bytes 409600 | tf_op jit(solution)/shard_map/dot_general | solution.py:33
  93.6 0.0 copy-done.6
  93.6 1.0 %fusion = f32[1024,32]{0,1:T(8,128)} fusion(f32[1024,32]{0,1:T(8,128)S(1)} %copy-done.6, f32[1024,32]{0,1:T(8,128)S(1)} %copy-done, f32[32,128]{1,0:T(8,128)S(1)} %get-tuple-element.5), kind=kOutput, calls=%fused_computation.2 | convolution fusion | flops 12615680 | bytes 409600 | tf_op jit(solution)/shard_map/dot_general | solution.py:33
  94.6 0.7 copy.11
  (2 shorter events, 0.0 us)
Async XLA Ops:
  0.6 0.7 copy-start.3
  1.4 0.7 copy-start.4
  1.4 0.7 copy-start.5
  2.1 0.9 copy-start
  3.0 0.9 copy-start.1
  3.9 0.8 copy-start.2
  92.5 1.1 %copy-start.6 = (f32[1024,32]{0,1:T(8,128)S(1)}, f32[1024,32]{0,1:T(8,128)}, u32[]{:S(2)}) copy-start(f32[1024,32]{0,1:T(8,128)} %param.8) | copy-start | bytes 393220

commit v2 on v1

v2 whole, which is shorter than its diff:
```python
import math

import jax
import jax.numpy as jnp
from jax import lax
from jax.experimental import pallas as pl
from jax.experimental.pallas import tpu as pltpu
from jax.sharding import PartitionSpec as P

D = 64
NRHS = 32
LEAF = 512
RANK = 128
NEAR = 4
FAR = 16
CPD = 1024
N_GX = 8
N_GY = 16
N_Y = 4
NODES = 255
FIRST = 127
AUG = D + 16
PAY = AUG + NRHS
LEAF_ROWS = D + NRHS
SCALE = math.log2(math.e) / D
FULL = lax.Precision.HIGHEST
F32, BF16 = jnp.float32, jnp.bfloat16
MESH = pl.DeviceIdType.MESH


def dot(a, b, contract=((1,), (0,)), precision=None):
    return lax.dot_general(a, b, (contract, ((), ())), precision=precision, preferred_element_type=F32)


def square_rows(wide):
    half = -0.5 * jnp.sum(wide * wide, axis=0, keepdims=True)
    high = half.astype(BF16).astype(F32)
    rest = half - high
    middle = rest.astype(BF16).astype(F32)
    low = rest - middle
    row = lax.broadcasted_iota(jnp.int32, (16, wide.shape[1]), 0)
    ones = jnp.where((row >= 4) & (row < 7), 1.0, 0.0)
    return jnp.where(row == 0, high, jnp.where(row == 1, middle, jnp.where(row == 2, low, ones)))


def turned(rows):
    return jnp.concatenate([pltpu.roll(rows[:8], 4, 0), rows[8:]], axis=0)


def kernel_body(
    points_in, residual_in, near_in, skeleton_in, upper_in, far_in,
    image, coeffs,
    points, residual, near, skeleton, upper, far,
    nodes, own, own_right, own_left, asked, stage, leaves, near_acc, far_acc, part1, part2,
    in_s, req_s, req_r, pay_s, pay_r, near_s, near_r, y_s, y_r, on_s, on_r, sib_s, sib_r,
    one_s, one_r, two_s, two_r,
):
    gx, gy = lax.axis_index("gx"), lax.axis_index("gy")
    y, core = gx // 2, gx % 2
    me = gx * N_GY + gy
    sibling = 2 * y + (1 - core)

    pairs = ((near_in, near), (skeleton_in, skeleton), (points_in, points), (residual_in, residual), (upper_in, upper), (far_in, far))
    loads = [pltpu.make_async_copy(a, b, in_s.at[i]) for i, (a, b) in enumerate(pairs)]
    for load in loads:
        load.start()

    barrier = pltpu.get_barrier_semaphore()

    @pl.loop(1, N_GY)
    def _(k):
        pl.semaphore_signal(barrier, inc=1, device_id=(gx, (gy + k) % N_GY), device_id_type=MESH)

    @pl.loop(1, N_GX)
    def _(k):
        pl.semaphore_signal(barrier, inc=1, device_id=((gx + k) % N_GX, gy), device_id_type=MESH)

    def copy(src, dst, send, recv, device):
        return pltpu.make_async_remote_copy(
            src_ref=src, dst_ref=dst, send_sem=send, recv_sem=recv, device_id=device, device_id_type=MESH
        )

    loads[0].wait()
    row = lax.broadcasted_iota(jnp.int32, (16, 128), 0)
    wanted = jnp.full((16, 128), -1, jnp.int32)
    for leaf in range(2):
        for n in range(NEAR):
            wanted = jnp.where(row == leaf * NEAR + n, near[leaf, n], wanted)
    asked[gy] = wanted.astype(F32).astype(BF16)
    for load in loads[1:]:
        load.wait()

    for leaf in range(2):
        at = pl.ds(leaf * LEAF, LEAF)
        wide = points[:, at].astype(F32)
        rows = square_rows(wide)
        own_right[leaf, 0:D] = points[:, at]
        own_right[leaf, D:AUG] = rows.astype(BF16)
        both = jnp.concatenate([wide, turned(rows), jnp.zeros((48, LEAF), F32)], axis=0)
        own_left[leaf] = both.T.astype(BF16)
        own[leaf, 0:D] = points[:, at]
        own[leaf, D:LEAF_ROWS] = residual[:, at].astype(BF16)
    pick = skeleton[...]
    skel = jnp.zeros((D, RANK), F32)
    for leaf in range(2):
        place = lax.broadcasted_iota(jnp.int32, (LEAF, RANK), 0) + leaf * LEAF
        skel += dot(points[:, pl.ds(leaf * LEAF, LEAF)], jnp.where(place == pick, 1.0, 0.0).astype(BF16))
    rows = square_rows(skel)
    left = jnp.concatenate([skel, turned(rows), jnp.zeros((48, RANK), F32)], axis=0).T.astype(BF16)
    weights = jnp.zeros((NRHS, RANK), F32)
    for leaf in range(2):
        tile = jnp.exp2(SCALE * dot(left[:, :AUG], own_right[leaf]))
        weights += dot(residual[:, pl.ds(leaf * LEAF, LEAF)], tile, ((1,), (1,)), FULL)
    mine = FIRST + me
    nodes[mine, 0:D] = skel.astype(BF16)
    nodes[mine, D:AUG] = rows.astype(BF16)
    nodes[mine, AUG:PAY] = (weights * (1.0 / math.sqrt(CPD))).astype(BF16)

    pl.semaphore_wait(barrier, N_GY - 1 + N_GX - 1)

    def req_copy(peer, slot):
        return copy(asked.at[gy], asked.at[slot], req_s.at[peer], req_r.at[slot], (gx, peer))

    def pay_copy(peer, slot):
        at = FIRST + gx * N_GY + slot
        return copy(nodes.at[mine], nodes.at[at], pay_s.at[peer], pay_r.at[slot], (gx, peer))

    def near_copy(peer, slot):
        return copy(stage.at[peer], leaves.at[slot], near_s.at[peer], near_r.at[slot], (gx, peer))

    @pl.loop(1, N_GY)
    def _(k):
        req_copy((gy + k) % N_GY, gy).start()

    @pl.loop(1, N_GY)
    def _(k):
        pay_copy((gy + k) % N_GY, gy).start()

    this = (2 * me + 1).astype(F32)
    leaves[gy] = own[0]

    @pl.loop(1, N_GY)
    def _(k):
        peer = (gy + k) % N_GY
        req_copy(peer, peer).wait_recv()
        second = jnp.where(asked[peer].astype(F32) == this, 1.0, 0.0)
        second = jnp.max(second, axis=0, keepdims=True)
        second = jnp.concatenate([second] * 4, axis=1)
        for r in range(0, LEAF_ROWS, 32):
            at = pl.ds(r, 32)
            stage[peer, at] = jnp.where(
                jnp.broadcast_to(second, (32, LEAF)) > 0.5, own[1, at].astype(F32), own[0, at].astype(F32)
            ).astype(BF16)
        near_copy(peer, gy).start()

    def tile_term(leaf, right, values):
        tile = jnp.exp2(SCALE * dot(own_left[leaf, :, :AUG], right)).astype(BF16)
        return dot(tile, values, ((1,), (1,)))

    @pl.loop(0, 2)
    def _(leaf):
        near_acc[leaf] = tile_term(leaf, own_right[leaf], own[leaf, D:LEAF_ROWS])

    @pl.loop(1, N_GY)
    def _(k):
        peer = (gy + k) % N_GY
        pay_copy(peer, peer).wait_recv()

    def half(row, h):
        return nodes.at[pl.ds(FIRST + row * N_GY + h * 8, 8)]

    def row_of(step, other=False):
        return 2 * ((y + step) % N_Y) + (1 - core if other else core)

    def y_copy(step, h, source):
        to = (row_of(step), gy)
        k = 0 if step == 1 else 1
        return copy(half(gx, h), half(row_of(source), h), y_s.at[k, h], y_r.at[k, h], to)

    def on_copy(step, source):
        h = k = 0 if step == 1 else 1
        return copy(half(row_of(-step), h), half(row_of(source), h), on_s.at[k], on_r.at[k], (row_of(step), gy))

    def sib_copy(step, h, other):
        at = (y + step) % N_Y
        return copy(half(row_of(step), h), half(row_of(step, other), h), sib_s.at[at, h], sib_r.at[at, h], (sibling, gy))

    for h in range(2):
        y_copy(1, h, 0).start()
        y_copy(-1, 1 - h, 0).start()
    for h in range(2):
        sib_copy(0, h, False).start()

    def build(first, count):
        done = []
        for i in range(count):
            u = first + i
            a, b = nodes[2 * u + 1], nodes[2 * u + 2]
            choice = jnp.broadcast_to(upper[pl.ds(u, 1), :], (AUG, RANK))
            lane = jnp.bitwise_and(choice, RANK - 1)
            from_a, from_b = (
                jnp.take_along_axis(x[:AUG].astype(F32), lane, axis=1, mode="promise_in_bounds") for x in (a, b)
            )
            right = jnp.where(choice < RANK, from_a, from_b)
            left = jnp.concatenate([right[:D], turned(right[D:])], axis=0).astype(BF16)
            both = jnp.concatenate([a, b], axis=1)
            tile = jnp.exp2(SCALE * dot(left, both[:AUG], ((0,), (0,)))).astype(BF16)
            sums = dot(both[D:], tile, ((1,), (1,)))
            done.append((right.astype(BF16), (sums[16:] / sums[4:5]).astype(BF16)))
        for i, (right, weights) in enumerate(done):
            nodes[first + i, 0:AUG] = right
            nodes[first + i, AUG:PAY] = weights

    def build_row(row):
        build(63 + row * 8, 8)
        build(31 + row * 4, 4)
        build(15 + row * 2, 2)
        build(7 + row, 1)

    def near_tile(n):
        leaf = n // NEAR
        got = leaves[(near[leaf, n % NEAR] // 2) % N_GY]
        right = jnp.concatenate([got[:D], square_rows(got[:D].astype(F32)).astype(BF16)], axis=0)
        near_acc[leaf] = near_acc[leaf] + tile_term(leaf, right, got[D:])

    @pl.loop(0, N_GX)
    def _(i):
        @pl.when(i == 1)
        def _():
            for step in (1, -1):
                h = 0 if step == 1 else 1
                y_copy(step, h, -step).wait_recv()
                on_copy(step, -step).start()
                sib_copy(-step, h, False).start()
            for h in range(2):
                sib_copy(0, h, True).wait_recv()

        @pl.when(i == 2)
        def _():
            for step in (-1, 1):
                h = 1 if step == 1 else 0
                y_copy(step, h, -step).wait_recv()
                sib_copy(-step, h, False).start()

        @pl.when(i == 3)
        def _():
            for h in range(2):
                sib_copy(1, h, True).wait_recv()

        @pl.when(i == 5)
        def _():
            for h in range(2):
                sib_copy(-1, h, True).wait_recv()

        @pl.when(i == 6)
        def _():
            for step in (1, -1):
                on_copy(step, 2).wait_recv()
                sib_copy(2, 0 if step == 1 else 1, False).start()

        @pl.when(i == 7)
        def _():
            @pl.loop(1, N_GY)
            def _(k):
                peer = (gy + k) % N_GY
                near_copy(peer, peer).wait_recv()

            pl.loop(0, 2 * NEAR)(near_tile)
            for h in range(2):
                sib_copy(2, h, True).wait_recv()

        turn = i // 2
        away = turn + turn // 2 - 2 * (turn // 3)
        build_row(2 * ((y + away) % N_Y) + (core + i % 2) % 2)

    build(3, 4)
    build(1, 2)
    build(0, 1)

    far_acc[...] = jnp.zeros_like(far_acc)

    @pl.loop(0, FAR // 2)
    def _(n):
        leaf, group = n // (FAR // 4), n % (FAR // 4)
        got = jnp.concatenate([nodes[far[leaf, 4 * group + i]] for i in range(4)], axis=1)
        far_acc[leaf] = far_acc[leaf] + tile_term(leaf, got[:AUG], got[AUG:])

    for leaf in range(2):
        at = pl.ds(leaf * LEAF, LEAF)
        terms = near_acc[leaf] * (1.0 / math.sqrt(LEAF)) + far_acc[leaf] * (1.0 / RANK)
        image[:, at] = residual[:, at] + terms.T

    both = jnp.concatenate([image[...], residual[...]], axis=0)
    gram = dot(image[...], both, ((1,), (1,)), FULL)
    part1[gy] = jnp.concatenate([gram[:16], gram[16:]], axis=1)

    def one_copy(peer, slot):
        return copy(part1.at[gy], part1.at[slot], one_s.at[peer], one_r.at[slot], (gx, peer))

    def two_copy(peer, slot):
        return copy(part2.at[gx], part2.at[slot], two_s.at[peer], two_r.at[slot], (peer, gy))

    @pl.loop(1, N_GY)
    def _(k):
        one_copy((gy + k) % N_GY, gy).start()

    @pl.loop(1, N_GY)
    def _(k):
        peer = (gy + k) % N_GY
        one_copy(peer, peer).wait_recv()

    total = part1[0]
    for k in range(1, N_GY):
        total += part1[k]
    part2[gx] = total

    @pl.loop(1, N_GX)
    def _(k):
        two_copy((gx + k) % N_GX, gx).start()

    @pl.loop(1, N_GX)
    def _(k):
        peer = (gx + k) % N_GX
        two_copy(peer, peer).wait_recv()

    total = part2[0]
    for k in range(1, N_GX):
        total += part2[k]

    work = jnp.concatenate([total, pltpu.roll(total, 64, 1)], axis=0)
    row = lax.broadcasted_iota(jnp.int32, (NRHS, 128), 0)
    for k in range(NRHS):
        pivot_row = work[k : k + 1] / work[k : k + 1, k : k + 1]
        work = jnp.where(row == k, pivot_row, work - work[:, k : k + 1] * pivot_row)
    coeffs[...] = work

    @pl.loop(1, N_GY)
    def _(k):
        peer = (gy + k) % N_GY
        req_copy(peer, gy).wait_send()
        pay_copy(peer, gy).wait_send()
        near_copy(peer, gy).wait_send()
        one_copy(peer, gy).wait_send()

    @pl.loop(1, N_GX)
    def _(k):
        two_copy((gx + k) % N_GX, gx).wait_send()

    for step in (1, -1):
        for h in range(2):
            y_copy(step, h, 0).wait_send()
        on_copy(step, -step).wait_send()
    for step in range(N_Y):
        for h in range(2):
            sib_copy(step, h, False).wait_send()


def shards(points, solution, residual, near_leaves, node_skeleton, upper_skeleton, far_nodes):
    vmem, hbm = (pl.BlockSpec(memory_space=m) for m in (pltpu.VMEM, pltpu.HBM))
    dma = pltpu.SemaphoreType.DMA
    residual_t = residual.T
    image_t, work = pl.pallas_call(
        kernel_body,
        out_shape=(
            jax.ShapeDtypeStruct((NRHS, CPD), F32),
            jax.ShapeDtypeStruct((NRHS, 128), F32),
        ),
        in_specs=[hbm] * 6,
        out_specs=(vmem, vmem),
        scratch_shapes=[
            pltpu.VMEM((D, CPD), BF16),
            pltpu.VMEM((NRHS, CPD), F32),
            pltpu.SMEM((2, NEAR), jnp.int32),
            pltpu.VMEM((1, RANK), jnp.int32),
            pltpu.VMEM((FIRST, RANK), jnp.int32),
            pltpu.SMEM((2, FAR), jnp.int32),
            pltpu.VMEM((NODES, PAY, RANK), BF16),
            pltpu.VMEM((2, LEAF_ROWS, LEAF), BF16),
            pltpu.VMEM((2, AUG, LEAF), BF16),
            pltpu.VMEM((2, LEAF, 128), BF16),
            pltpu.VMEM((N_GY, 16, 128), BF16),
            pltpu.VMEM((N_GY, LEAF_ROWS, LEAF), BF16),
            pltpu.VMEM((N_GY, LEAF_ROWS, LEAF), BF16),
            pltpu.VMEM((2, LEAF, NRHS), F32),
            pltpu.VMEM((2, LEAF, NRHS), F32),
            pltpu.VMEM((N_GY, 16, 128), F32),
            pltpu.VMEM((N_GX, 16, 128), F32),
            dma((6,)),
            dma((N_GY,)), dma((N_GY,)), dma((N_GY,)), dma((N_GY,)), dma((N_GY,)), dma((N_GY,)),
            dma((2, 2)), dma((2, 2)), dma((2,)), dma((2,)), dma((N_Y, 2)), dma((N_Y, 2)),
            dma((N_GY,)), dma((N_GY,)), dma((N_GX,)), dma((N_GX,)),
        ],
        compiler_params=pltpu.CompilerParams(
            collective_id=0, has_side_effects=True, vmem_limit_bytes=48 * 2**20
        ),
    )(points.T, residual_t, near_leaves, node_skeleton, upper_skeleton, far_nodes)
    step = work[:, NRHS : 2 * NRHS]
    solution_next = solution.T + dot(step, residual_t, ((0,), (0,)), FULL)
    residual_next = residual_t - dot(step, image_t, ((0,), (0,)), FULL)
    return solution_next.T, residual_next.T, image_t.T


def solution(mesh):
    split = P(("gx", "gy"), None)
    return jax.shard_map(
        shards,
        mesh=mesh,
        in_specs=(split, split, split, split, split, P(), split),
        out_specs=(split, split, split),
        check_vma=False,
    )
```

time: 95.5 us -> 73.5 us (0.77)
  Pallas kernels: 87.8 us -> 66.6 us
    pallas_call x1, Pallas kernels: 87.8 us -> 66.6 us  [shards(): pl.pallas_call(kernel_body, out_shape=(jax.ShapeDtypeStruct((NRHS, CPD),...]
where the time goes in v2:
time: 73.5 us; the launch traced here: 73.3 us
  Pallas kernels  66.6 us (91%)
  local copies, waits for them, and re-layouts  3.98 us (5%)
  matrix products  2.08 us (3%)
    pallas_call x1, Pallas kernels, shards(): pl.pallas_call(kernel_body, out_shape=(jax.ShapeDtypeStruct((NRHS, CPD),...  66.6 us
    unnamed x15, local copies, waits for them, and re-layouts  3.98 us
    dot_general x2, matrix products, dot(): lax.dot_general(a, b, (contract, ((), ())), precision=precision, preferre...  2.08 us

profile of v2, /device:TPU:1, one launch (start us, length us, event | category | flops | bytes accessed | tf_op | source)
XLA Modules:
  0.0 73.3 jit_solution(6943197586794201554)
XLA Ops:
  0.6 0.0 copy-start.4
  0.6 0.0 copy-start.3
  0.7 0.0 copy-start.5
  0.7 0.7 copy-done.4
  1.3 0.0 copy-done.3
  1.3 0.0 copy-done.5
  1.3 0.0 copy-start
  1.3 0.9 %copy-done = f32[1024,32]{0,1:T(8,128)S(1)} copy-done((f32[1024,32]{0,1:T(8,128)S(1)}, f32[1024,32]{0,1:T(8,128)}, u32[]{:S(2)}) %copy-start) | copy-done | bytes 131096
  2.2 0.0 copy-start.1
  2.2 0.9 %copy-done.1 = bf16[1024,64]{0,1:T(8,128)(2,1)S(1)} copy-done((bf16[1024,64]{0,1:T(8,128)(2,1)S(1)}, bf16[1024,64]{0,1:T(8,128)(2,1)}, u32[]{:S(2)}) %copy-start.1) | copy-done | bytes 131096
  3.1 0.0 copy-start.2
  3.1 0.8 %copy-done.2 = s32[127,128]{1,0:T(8,128)S(1)} copy-done((s32[127,128]{1,0:T(8,128)S(1)}, s32[127,128]{1,0:T(8,128)}, u32[]{:S(2)}) %copy-start.2) | copy-done | bytes 65048
  4.0 66.6 %shard_map.94 = (f32[32,1024]{1,0:T(8,128)S(1)}, f32[32,128]{1,0:T(8,128)S(1)}) custom-call(bf16[64,1024]{1,0:T(8,128)(2,1)S(1)} %bitcast.11, f32[32,1024]{1,0:T(8,128)S(1)} %bitcast.9, s32[2,4]{1,0:T(2,128)S(1)} %copy-done.3, s32[1,128]{1,0:T(1,128)S(1)} %copy-done.5, s32[127,128]{1,0:T(8,128)S(1)} %copy-done.2, s32[2,16]{1,0:T(2,128)S(1)} %copy-done.4), custom_call_target="tpu_custom_call" | custom-call | tf_op jit(solution)/shard_map/pallas_call | solution.py:362
  70.6 0.0 copy-start.6
  70.6 1.0 %convolution_subtract_fusion = f32[1024,32]{0,1:T(8,128)} fusion(f32[1024,32]{0,1:T(8,128)S(1)} %copy-done, f32[32,1024]{1,0:T(8,128)S(1)} %get-tuple-element.6, f32[32,128]{1,0:T(8,128)S(1)} %get-tuple-element.5), kind=kOutput, calls=%fused_computation | convolution fusion | flops 12615680 | bytes 409600 | tf_op jit(solution)/shard_map/dot_general | solution.py:32
  71.6 0.0 copy-done.6
  71.6 1.0 %fusion = f32[1024,32]{0,1:T(8,128)} fusion(f32[1024,32]{0,1:T(8,128)S(1)} %copy-done.6, f32[1024,32]{0,1:T(8,128)S(1)} %copy-done, f32[32,128]{1,0:T(8,128)S(1)} %get-tuple-element.5), kind=kOutput, calls=%fused_computation.2 | convolution fusion | flops 12615680 | bytes 409600 | tf_op jit(solution)/shard_map/dot_general | solution.py:32
  72.7 0.7 copy.11
Async XLA Ops:
  0.6 0.7 copy-start.4
  0.6 0.7 copy-start.3
  0.7 0.7 copy-start.5
  1.3 0.9 %copy-start = (f32[1024,32]{0,1:T(8,128)S(1)}, f32[1024,32]{0,1:T(8,128)}, u32[]{:S(2)}) copy-start(f32[1024,32]{0,1:T(8,128)} %param.9) | copy-start | bytes 393220
  2.2 0.9 %copy-start.1 = (bf16[1024,64]{0,1:T(8,128)(2,1)S(1)}, bf16[1024,64]{0,1:T(8,128)(2,1)}, u32[]{:S(2)}) copy-start(bf16[1024,64]{0,1:T(8,128)(2,1)} %param.7) | copy-start | bytes 393220
  3.1 0.8 %copy-start.2 = (s32[127,128]{1,0:T(8,128)S(1)}, s32[127,128]{1,0:T(8,128)}, u32[]{:S(2)}) copy-start(s32[127,128]{1,0:T(8,128)} %upper_in.1) | copy-start | bytes 195076
  70.6 1.1 %copy-start.6 = (f32[1024,32]{0,1:T(8,128)S(1)}, f32[1024,32]{0,1:T(8,128)}, u32[]{:S(2)}) copy-start(f32[1024,32]{0,1:T(8,128)} %param.8) | copy-start | bytes 393220

commit v3 on v2

--- a/solution.py
+++ b/solution.py
@@ -90,8 +90,9 @@
     for load in loads[1:]:
         load.wait()
 
-    for leaf in range(2):
-        at = pl.ds(leaf * LEAF, LEAF)
+    @pl.loop(0, 2)
+    def _(leaf):
+        at = pl.ds(pl.multiple_of(leaf * LEAF, LEAF), LEAF)
         wide = points[:, at].astype(F32)
         rows = square_rows(wide)
         own_right[leaf, 0:D] = points[:, at]
@@ -100,11 +101,9 @@
         own_left[leaf] = both.T.astype(BF16)
         own[leaf, 0:D] = points[:, at]
         own[leaf, D:LEAF_ROWS] = residual[:, at].astype(BF16)
-    pick = skeleton[...]
-    skel = jnp.zeros((D, RANK), F32)
-    for leaf in range(2):
-        place = lax.broadcasted_iota(jnp.int32, (LEAF, RANK), 0) + leaf * LEAF
-        skel += dot(points[:, pl.ds(leaf * LEAF, LEAF)], jnp.where(place == pick, 1.0, 0.0).astype(BF16))
+
+    place = lax.broadcasted_iota(jnp.int32, (CPD, RANK), 0)
+    skel = dot(points[...], jnp.where(place == skeleton[...], 1.0, 0.0).astype(BF16))
     rows = square_rows(skel)
     left = jnp.concatenate([skel, turned(rows), jnp.zeros((48, RANK), F32)], axis=0).T.astype(BF16)
     weights = jnp.zeros((NRHS, RANK), F32)
@@ -218,8 +217,9 @@
         build(7 + row, 1)
 
     def near_tile(n):
-        leaf = n // NEAR
-        got = leaves[(near[leaf, n % NEAR] // 2) % N_GY]
+        leaf, pair = n // (NEAR // 2), n % (NEAR // 2)
+        got = [leaves[(near[leaf, 2 * pair + i] // 2) % N_GY] for i in range(2)]
+        got = jnp.concatenate(got, axis=1)
         right = jnp.concatenate([got[:D], square_rows(got[:D].astype(F32)).astype(BF16)], axis=0)
         near_acc[leaf] = near_acc[leaf] + tile_term(leaf, right, got[D:])
 
@@ -260,12 +260,6 @@
 
         @pl.when(i == 7)
         def _():
-            @pl.loop(1, N_GY)
-            def _(k):
-                peer = (gy + k) % N_GY
-                near_copy(peer, peer).wait_recv()
-
-            pl.loop(0, 2 * NEAR)(near_tile)
             for h in range(2):
                 sib_copy(2, h, True).wait_recv()
 
@@ -279,11 +273,18 @@
 
     far_acc[...] = jnp.zeros_like(far_acc)
 
-    @pl.loop(0, FAR // 2)
+    @pl.loop(0, FAR // 4)
     def _(n):
-        leaf, group = n // (FAR // 4), n % (FAR // 4)
-        got = jnp.concatenate([nodes[far[leaf, 4 * group + i]] for i in range(4)], axis=1)
+        leaf, group = n // (FAR // 8), n % (FAR // 8)
+        got = jnp.concatenate([nodes[far[leaf, 8 * group + i]] for i in range(8)], axis=1)
         far_acc[leaf] = far_acc[leaf] + tile_term(leaf, got[:AUG], got[AUG:])
+
+    @pl.loop(1, N_GY)
+    def _(k):
+        peer = (gy + k) % N_GY
+        near_copy(peer, peer).wait_recv()
+
+    pl.loop(0, NEAR)(near_tile)
 
     for leaf in range(2):
         at = pl.ds(leaf * LEAF, LEAF)
@@ -329,9 +330,20 @@
 
     work = jnp.concatenate([total, pltpu.roll(total, 64, 1)], axis=0)
     row = lax.broadcasted_iota(jnp.int32, (NRHS, 128), 0)
-    for k in range(NRHS):
-        pivot_row = work[k : k + 1] / work[k : k + 1, k : k + 1]
-        work = jnp.where(row == k, pivot_row, work - work[:, k : k + 1] * pivot_row)
+
+    def eight(_, work):
+        for k in range(0, 8, 2):
+            first, second = (jnp.broadcast_to(work[:, k + i : k + i + 1], (NRHS, 128)) for i in range(2))
+            inverse = 1.0 / first[k : k + 1]
+            factor = first[k + 1 : k + 2] * inverse
+            below = 1.0 / (second[k + 1 : k + 2] - factor * second[k : k + 1])
+            lower = (work[k + 1 : k + 2] - factor * work[k : k + 1]) * below
+            upper_row = (work[k : k + 1] - second[k : k + 1] * lower) * inverse
+            rest = work - first * upper_row - second * lower
+            work = jnp.where(row == k, upper_row, jnp.where(row == k + 1, lower, rest))
+        return pltpu.roll(jnp.concatenate([work[8:], work[:8]], axis=0), 120, 1)
+
+    work = lax.fori_loop(0, NRHS // 8, eight, work)
     coeffs[...] = work
 
     @pl.loop(1, N_GY)
@@ -353,6 +365,13 @@
     for step in range(N_Y):
         for h in range(2):
             sib_copy(step, h, False).wait_send()
+
+
+def update_body(work, solution, residual, image, solution_next, residual_next, image_out):
+    step = work[:, :NRHS].T
+    solution_next[...] = solution[...] + dot(step, residual[...], precision=FULL)
+    residual_next[...] = residual[...] - dot(step, image[...], precision=FULL)
+    image_out[...] = image[...]
 
 
 def shards(points, solution, residual, near_leaves, node_skeleton, upper_skeleton, far_nodes):
@@ -391,13 +410,16 @@
             dma((N_GY,)), dma((N_GY,)), dma((N_GX,)), dma((N_GX,)),
         ],
         compiler_params=pltpu.CompilerParams(
-            collective_id=0, has_side_effects=True, vmem_limit_bytes=48 * 2**20
+            collective_id=0, has_side_effects=True, vmem_limit_bytes=60 * 2**20
         ),
     )(points.T, residual_t, near_leaves, node_skeleton, upper_skeleton, far_nodes)
-    step = work[:, NRHS : 2 * NRHS]
-    solution_next = solution.T + dot(step, residual_t, ((0,), (0,)), FULL)
-    residual_next = residual_t - dot(step, image_t, ((0,), (0,)), FULL)
-    return solution_next.T, residual_next.T, image_t.T
+    outs = pl.pallas_call(
+        update_body,
+        out_shape=(jax.ShapeDtypeStruct((NRHS, CPD), F32),) * 3,
+        in_specs=[vmem] * 4,
+        out_specs=(vmem,) * 3,
+    )(work, solution.T, residual_t, image_t)
+    return tuple(o.T for o in outs)
 
 
 def solution(mesh):

time: 73.5 us -> 68 us (0.925)
  local copies, waits for them, and re-layouts: 3.98 us -> 0 us
  matrix products: 2.08 us -> 0 us
    unnamed x15 -> x0, local copies, waits for them, and re-layouts: 3.98 us -> none
    pallas_call x0 -> x1, Pallas kernels: none -> 2.16 us  [shards(): pl.pallas_call(update_body, out_shape=(jax.ShapeDtypeStruct((NRHS, CPD),...]
    dot_general x2 -> x0, matrix products: 2.08 us -> none  [dot(): lax.dot_general(a, b, (contract, ((), ())), precision=precision, preferre...]
    pallas_call x1, Pallas kernels: 66.6 us -> 65.1 us  [shards(): pl.pallas_call(kernel_body, out_shape=(jax.ShapeDtypeStruct((NRHS, CPD),...]
where the time goes in v3:
time: 68 us; the launch traced here: 67.9 us
  Pallas kernels  67.2 us (99%)
    pallas_call x1, Pallas kernels, shards(): pl.pallas_call(kernel_body, out_shape=(jax.ShapeDtypeStruct((NRHS, CPD),...  65.1 us
    pallas_call x1, Pallas kernels, shards(): pl.pallas_call(update_body, out_shape=(jax.ShapeDtypeStruct((NRHS, CPD),...  2.16 us

profile of v3, /device:TPU:1, one launch (start us, length us, event | category | flops | bytes accessed | tf_op | source)
XLA Modules:
  0.0 67.9 jit_solution(14813498459220069009)
XLA Ops:
  0.6 65.1 %shard_map.94 = (f32[32,1024]{1,0:T(8,128)}, f32[32,128]{1,0:T(8,128)}) custom-call(bf16[64,1024]{1,0:T(8,128)(2,1)} %bitcast.8, f32[32,1024]{1,0:T(8,128)} %bitcast.6, s32[2,4]{1,0:T(2,128)} %near_in.1, s32[1,128]{1,0:T(1,128)} %skeleton_in.1, s32[127,128]{1,0:T(8,128)} %upper_in.1, s32[2,16]{1,0:T(2,128)} %far_in.1), custom_call_target="tpu_custom_call" | custom-call | tf_op jit(solution)/shard_map/pallas_call | solution.py:381
  65.7 2.2 %shard_map.95 = (f32[32,1024]{1,0:T(8,128)}, f32[32,1024]{1,0:T(8,128)}, f32[32,1024]{1,0:T(8,128)}) custom-call(f32[32,128]{1,0:T(8,128)} %get-tuple-element.8.work, f32[32,1024]{1,0:T(8,128)} %bitcast.9, f32[32,1024]{1,0:T(8,128)} %bitcast.7, f32[32,1024]{1,0:T(8,128)} %get-tuple-element.9.image), custom_call_target="tpu_custom_call" | custom-call | tf_op jit(solution)/shard_map/pallas_call | solution.py:416

commit v4 on v3

--- a/solution.py
+++ b/solution.py
@@ -20,7 +20,8 @@
 NODES = 255
 FIRST = 127
 AUG = D + 16
-PAY = AUG + NRHS
+SENT = D + NRHS
+PAY = SENT + 16
 LEAF_ROWS = D + NRHS
 SCALE = math.log2(math.e) / D
 FULL = lax.Precision.HIGHEST
@@ -112,8 +113,7 @@
         weights += dot(residual[:, pl.ds(leaf * LEAF, LEAF)], tile, ((1,), (1,)), FULL)
     mine = FIRST + me
     nodes[mine, 0:D] = skel.astype(BF16)
-    nodes[mine, D:AUG] = rows.astype(BF16)
-    nodes[mine, AUG:PAY] = (weights * (1.0 / math.sqrt(CPD))).astype(BF16)
+    nodes[mine, D:SENT] = (weights * (1.0 / math.sqrt(CPD))).astype(BF16)
 
     pl.semaphore_wait(barrier, N_GY - 1 + N_GX - 1)
 
@@ -122,7 +122,7 @@
 
     def pay_copy(peer, slot):
         at = FIRST + gx * N_GY + slot
-        return copy(nodes.at[mine], nodes.at[at], pay_s.at[peer], pay_r.at[slot], (gx, peer))
+        return copy(nodes.at[mine, pl.ds(0, SENT)], nodes.at[at, pl.ds(0, SENT)], pay_s.at[peer], pay_r.at[slot], (gx, peer))
 
     def near_copy(peer, slot):
         return copy(stage.at[peer], leaves.at[slot], near_s.at[peer], near_r.at[slot], (gx, peer))
@@ -134,6 +134,44 @@
     @pl.loop(1, N_GY)
     def _(k):
         pay_copy((gy + k) % N_GY, gy).start()
+
+    def tile_term(leaf, right, values):
+        tile = jnp.exp2(SCALE * dot(own_left[leaf, :, :AUG], right)).astype(BF16)
+        return dot(tile, values, ((1,), (1,)))
+
+    @pl.loop(0, 2)
+    def _(leaf):
+        near_acc[leaf] = tile_term(leaf, own_right[leaf], own[leaf, D:LEAF_ROWS])
+
+    @pl.loop(1, N_GY)
+    def _(k):
+        peer = (gy + k) % N_GY
+        pay_copy(peer, peer).wait_recv()
+
+    def half(row, h):
+        return nodes.at[pl.ds(FIRST + row * N_GY + h * 8, 8), pl.ds(0, SENT)]
+
+    def row_of(step, other=False):
+        return 2 * ((y + step) % N_Y) + (1 - core if other else core)
+
+    def y_copy(step, h, source):
+        to = (row_of(step), gy)
+        k = 0 if step == 1 else 1
+        return copy(half(gx, h), half(row_of(source), h), y_s.at[k, h], y_r.at[k, h], to)
+
+    def on_copy(step, source):
+        h = k = 0 if step == 1 else 1
+        return copy(half(row_of(-step), h), half(row_of(source), h), on_s.at[k], on_r.at[k], (row_of(step), gy))
+
+    def sib_copy(step, h, other):
+        at = (y + step) % N_Y
+        return copy(half(row_of(step), h), half(row_of(step, other), h), sib_s.at[at, h], sib_r.at[at, h], (sibling, gy))
+
+    for h in range(2):
+        y_copy(1, h, 0).start()
+        y_copy(-1, 1 - h, 0).start()
+    for h in range(2):
+        sib_copy(0, h, False).start()
 
     this = (2 * me + 1).astype(F32)
     leaves[gy] = own[0]
@@ -152,43 +190,8 @@
             ).astype(BF16)
         near_copy(peer, gy).start()
 
-    def tile_term(leaf, right, values):
-        tile = jnp.exp2(SCALE * dot(own_left[leaf, :, :AUG], right)).astype(BF16)
-        return dot(tile, values, ((1,), (1,)))
-
-    @pl.loop(0, 2)
-    def _(leaf):
-        near_acc[leaf] = tile_term(leaf, own_right[leaf], own[leaf, D:LEAF_ROWS])
-
-    @pl.loop(1, N_GY)
-    def _(k):
-        peer = (gy + k) % N_GY
-        pay_copy(peer, peer).wait_recv()
-
-    def half(row, h):
-        return nodes.at[pl.ds(FIRST + row * N_GY + h * 8, 8)]
-
-    def row_of(step, other=False):
-        return 2 * ((y + step) % N_Y) + (1 - core if other else core)
-
-    def y_copy(step, h, source):
-        to = (row_of(step), gy)
-        k = 0 if step == 1 else 1
-        return copy(half(gx, h), half(row_of(source), h), y_s.at[k, h], y_r.at[k, h], to)
-
-    def on_copy(step, source):
-        h = k = 0 if step == 1 else 1
-        return copy(half(row_of(-step), h), half(row_of(source), h), on_s.at[k], on_r.at[k], (row_of(step), gy))
-
-    def sib_copy(step, h, other):
-        at = (y + step) % N_Y
-        return copy(half(row_of(step), h), half(row_of(step, other), h), sib_s.at[at, h], sib_r.at[at, h], (sibling, gy))
-
-    for h in range(2):
-        y_copy(1, h, 0).start()
-        y_copy(-1, 1 - h, 0).start()
-    for h in range(2):
-        sib_copy(0, h, False).start()
+    def right_of(node):
+        return jnp.concatenate([node[:D], node[SENT:]], axis=0)
 
     def build(first, count):
         done = []
@@ -198,19 +201,25 @@
             choice = jnp.broadcast_to(upper[pl.ds(u, 1), :], (AUG, RANK))
             lane = jnp.bitwise_and(choice, RANK - 1)
             from_a, from_b = (
-                jnp.take_along_axis(x[:AUG].astype(F32), lane, axis=1, mode="promise_in_bounds") for x in (a, b)
+                jnp.take_along_axis(right_of(x).astype(F32), lane, axis=1, mode="promise_in_bounds") for x in (a, b)
             )
             right = jnp.where(choice < RANK, from_a, from_b)
             left = jnp.concatenate([right[:D], turned(right[D:])], axis=0).astype(BF16)
             both = jnp.concatenate([a, b], axis=1)
-            tile = jnp.exp2(SCALE * dot(left, both[:AUG], ((0,), (0,)))).astype(BF16)
+            tile = jnp.exp2(SCALE * dot(left, right_of(both), ((0,), (0,)))).astype(BF16)
             sums = dot(both[D:], tile, ((1,), (1,)))
-            done.append((right.astype(BF16), (sums[16:] / sums[4:5]).astype(BF16)))
-        for i, (right, weights) in enumerate(done):
-            nodes[first + i, 0:AUG] = right
-            nodes[first + i, AUG:PAY] = weights
+            weights = sums[:NRHS] / sums[NRHS + 4 : NRHS + 5]
+            done.append(jnp.concatenate([right[:D], weights, right[D:]], axis=0).astype(BF16))
+        for i, node in enumerate(done):
+            nodes[first + i] = node
 
     def build_row(row):
+        for h in range(2):
+            first = FIRST + row * N_GY + h * 8
+            wide = jnp.concatenate([nodes[first + i, 0:D].astype(F32) for i in range(8)], axis=1)
+            rows = square_rows(wide).astype(BF16)
+            for i in range(8):
+                nodes[first + i, SENT:PAY] = rows[:, i * RANK : (i + 1) * RANK]
         build(63 + row * 8, 8)
         build(31 + row * 4, 4)
         build(15 + row * 2, 2)
@@ -277,7 +286,7 @@
     def _(n):
         leaf, group = n // (FAR // 8), n % (FAR // 8)
         got = jnp.concatenate([nodes[far[leaf, 8 * group + i]] for i in range(8)], axis=1)
-        far_acc[leaf] = far_acc[leaf] + tile_term(leaf, got[:AUG], got[AUG:])
+        far_acc[leaf] = far_acc[leaf] + tile_term(leaf, right_of(got), got[D:SENT])
 
     @pl.loop(1, N_GY)
     def _(k):

time: 68 us -> 60.4 us (0.89)
  Pallas kernels: 67.2 us -> 59.7 us
    pallas_call x1, Pallas kernels: 65.1 us -> 57.5 us  [shards(): pl.pallas_call(kernel_body, out_shape=(jax.ShapeDtypeStruct((NRHS, CPD),...]
where the time goes in v4:
time: 60.4 us; the launch traced here: 60.3 us
  Pallas kernels  59.7 us (99%)
  between operations  0.64 us (1%)
    pallas_call x1, Pallas kernels, shards(): pl.pallas_call(kernel_body, out_shape=(jax.ShapeDtypeStruct((NRHS, CPD),...  57.5 us
    pallas_call x1, Pallas kernels, shards(): pl.pallas_call(update_body, out_shape=(jax.ShapeDtypeStruct((NRHS, CPD),...  2.17 us

profile of v4, /device:TPU:1, one launch (start us, length us, event | category | flops | bytes accessed | tf_op | source)
XLA Modules:
  0.0 60.3 jit_solution(11932769253020141303)
XLA Ops:
  0.6 57.5 %shard_map.94 = (f32[32,1024]{1,0:T(8,128)}, f32[32,128]{1,0:T(8,128)}) custom-call(bf16[64,1024]{1,0:T(8,128)(2,1)} %bitcast.8, f32[32,1024]{1,0:T(8,128)} %bitcast.6, s32[2,4]{1,0:T(2,128)} %near_in.1, s32[1,128]{1,0:T(1,128)} %skeleton_in.1, s32[127,128]{1,0:T(8,128)} %upper_in.1, s32[2,16]{1,0:T(2,128)} %far_in.1), custom_call_target="tpu_custom_call" | custom-call | tf_op jit(solution)/shard_map/pallas_call | solution.py:390
  58.1 2.2 %shard_map.95 = (f32[32,1024]{1,0:T(8,128)}, f32[32,1024]{1,0:T(8,128)}, f32[32,1024]{1,0:T(8,128)}) custom-call(f32[32,128]{1,0:T(8,128)} %get-tuple-element.8.work, f32[32,1024]{1,0:T(8,128)} %bitcast.9, f32[32,1024]{1,0:T(8,128)} %bitcast.7, f32[32,1024]{1,0:T(8,128)} %get-tuple-element.9.image), custom_call_target="tpu_custom_call" | custom-call | tf_op jit(solution)/shard_map/pallas_call | solution.py:425

commit v5 on v4

--- a/solution.py
+++ b/solution.py
@@ -53,7 +53,7 @@
     image, coeffs,
     points, residual, near, skeleton, upper, far,
     nodes, own, own_right, own_left, asked, stage, leaves, near_acc, far_acc, part1, part2,
-    in_s, req_s, req_r, pay_s, pay_r, near_s, near_r, y_s, y_r, on_s, on_r, sib_s, sib_r,
+    in_s, req_s, req_r, pay_s, pay_r, near_s, near_r, y_s, y_r, on_s, on_r, sib_s, sib_r, full_s, full_r,
     one_s, one_r, two_s, two_r,
 ):
     gx, gy = lax.axis_index("gx"), lax.axis_index("gy")
@@ -163,15 +163,12 @@
         h = k = 0 if step == 1 else 1
         return copy(half(row_of(-step), h), half(row_of(source), h), on_s.at[k], on_r.at[k], (row_of(step), gy))
 
-    def sib_copy(step, h, other):
-        at = (y + step) % N_Y
-        return copy(half(row_of(step), h), half(row_of(step, other), h), sib_s.at[at, h], sib_r.at[at, h], (sibling, gy))
+    def sib_copy(h, other):
+        return copy(half(row_of(2), h), half(row_of(2, other), h), sib_s.at[h], sib_r.at[h], (sibling, gy))
 
     for h in range(2):
         y_copy(1, h, 0).start()
         y_copy(-1, 1 - h, 0).start()
-    for h in range(2):
-        sib_copy(0, h, False).start()
 
     this = (2 * me + 1).astype(F32)
     leaves[gy] = own[0]
@@ -232,7 +229,15 @@
         right = jnp.concatenate([got[:D], square_rows(got[:D].astype(F32)).astype(BF16)], axis=0)
         near_acc[leaf] = near_acc[leaf] + tile_term(leaf, right, got[D:])
 
-    @pl.loop(0, N_GX)
+    def run(row, level):
+        return nodes.at[pl.ds(2**level - 1 + row * (2**level // N_GX), 2**level // N_GX)]
+
+    def full_copy(step, level, other):
+        at = (y + step) % N_Y
+        send, recv = full_s.at[at, level - 3], full_r.at[at, level - 3]
+        return copy(run(row_of(step), level), run(row_of(step, other), level), send, recv, (sibling, gy))
+
+    @pl.loop(0, N_Y + 1)
     def _(i):
         @pl.when(i == 1)
         def _():
@@ -240,41 +245,35 @@
                 h = 0 if step == 1 else 1
                 y_copy(step, h, -step).wait_recv()
                 on_copy(step, -step).start()
-                sib_copy(-step, h, False).start()
-            for h in range(2):
-                sib_copy(0, h, True).wait_recv()
+            y_copy(-1, 0, 1).wait_recv()
 
         @pl.when(i == 2)
         def _():
-            for step in (-1, 1):
-                h = 1 if step == 1 else 0
-                y_copy(step, h, -step).wait_recv()
-                sib_copy(-step, h, False).start()
+            y_copy(1, 1, -1).wait_recv()
 
         @pl.when(i == 3)
-        def _():
-            for h in range(2):
-                sib_copy(1, h, True).wait_recv()
-
-        @pl.when(i == 5)
-        def _():
-            for h in range(2):
-                sib_copy(-1, h, True).wait_recv()
-
-        @pl.when(i == 6)
         def _():
             for step in (1, -1):
                 on_copy(step, 2).wait_recv()
-                sib_copy(2, 0 if step == 1 else 1, False).start()
-
-        @pl.when(i == 7)
+                sib_copy(0 if step == 1 else 1, False).start()
+
+        @pl.when(i == 4)
         def _():
             for h in range(2):
-                sib_copy(2, h, True).wait_recv()
-
-        turn = i // 2
+                sib_copy(h, True).wait_recv()
+
+        turn = i - i // N_Y
         away = turn + turn // 2 - 2 * (turn // 3)
-        build_row(2 * ((y + away) % N_Y) + (core + i % 2) % 2)
+        build_row(2 * ((y + away) % N_Y) + (core + i // N_Y) % 2)
+
+        @pl.when(i < 3)
+        def _():
+            for level in range(7, 2, -1):
+                full_copy(away, level, False).start()
+
+    for step in (0, 1, -1):
+        for level in range(7, 2, -1):
+            full_copy(step, level, True).wait_recv()
 
     build(3, 4)
     build(1, 2)
@@ -317,6 +316,25 @@
     @pl.loop(1, N_GY)
     def _(k):
         peer = (gy + k) % N_GY
+        req_copy(peer, gy).wait_send()
+        pay_copy(peer, gy).wait_send()
+        near_copy(peer, gy).wait_send()
+
+    for step in (1, -1):
+        for h in range(2):
+            y_copy(step, h, 0).wait_send()
+        on_copy(step, -step).wait_send()
+    for h in range(2):
+        sib_copy(h, False).wait_send()
+
+    @pl.loop(0, 3)
+    def _(i):
+        for level in range(7, 2, -1):
+            full_copy(i - 1, level, False).wait_send()
+
+    @pl.loop(1, N_GY)
+    def _(k):
+        peer = (gy + k) % N_GY
         one_copy(peer, peer).wait_recv()
 
     total = part1[0]
@@ -327,6 +345,10 @@
     @pl.loop(1, N_GX)
     def _(k):
         two_copy((gx + k) % N_GX, gx).start()
+
+    @pl.loop(1, N_GY)
+    def _(k):
+        one_copy((gy + k) % N_GY, gy).wait_send()
 
     @pl.loop(1, N_GX)
     def _(k):
@@ -355,25 +377,9 @@
     work = lax.fori_loop(0, NRHS // 8, eight, work)
     coeffs[...] = work
 
-    @pl.loop(1, N_GY)
-    def _(k):
-        peer = (gy + k) % N_GY
-        req_copy(peer, gy).wait_send()
-        pay_copy(peer, gy).wait_send()
-        near_copy(peer, gy).wait_send()
-        one_copy(peer, gy).wait_send()
-
     @pl.loop(1, N_GX)
     def _(k):
         two_copy((gx + k) % N_GX, gx).wait_send()
-
-    for step in (1, -1):
-        for h in range(2):
-            y_copy(step, h, 0).wait_send()
-        on_copy(step, -step).wait_send()
-    for step in range(N_Y):
-        for h in range(2):
-            sib_copy(step, h, False).wait_send()
 
 
 def update_body(work, solution, residual, image, solution_next, residual_next, image_out):
@@ -415,7 +421,7 @@
             pltpu.VMEM((N_GX, 16, 128), F32),
             dma((6,)),
             dma((N_GY,)), dma((N_GY,)), dma((N_GY,)), dma((N_GY,)), dma((N_GY,)), dma((N_GY,)),
-            dma((2, 2)), dma((2, 2)), dma((2,)), dma((2,)), dma((N_Y, 2)), dma((N_Y, 2)),
+            dma((2, 2)), dma((2, 2)), dma((2,)), dma((2,)), dma((2,)), dma((2,)), dma((N_Y, 5)), dma((N_Y, 5)),
             dma((N_GY,)), dma((N_GY,)), dma((N_GX,)), dma((N_GX,)),
         ],
         compiler_params=pltpu.CompilerParams(

time: 60.4 us -> 58.5 us (0.969)
  Pallas kernels: 59.7 us -> 57.7 us
    pallas_call x1, Pallas kernels: 57.5 us -> 55.5 us  [shards(): pl.pallas_call(kernel_body, out_shape=(jax.ShapeDtypeStruct((NRHS, CPD),...]
where the time goes in v5:
time: 58.5 us; the launch traced here: 58.3 us
  Pallas kernels  57.7 us (99%)
  between operations  0.64 us (1%)
    pallas_call x1, Pallas kernels, shards(): pl.pallas_call(kernel_body, out_shape=(jax.ShapeDtypeStruct((NRHS, CPD),...  55.5 us
    pallas_call x1, Pallas kernels, shards(): pl.pallas_call(update_body, out_shape=(jax.ShapeDtypeStruct((NRHS, CPD),...  2.16 us

profile of v5, /device:TPU:1, one launch (start us, length us, event | category | flops | bytes accessed | tf_op | source)
XLA Modules:
  0.0 58.3 jit_solution(13402111538147630945)
XLA Ops:
  0.6 55.5 %shard_map.94 = (f32[32,1024]{1,0:T(8,128)}, f32[32,128]{1,0:T(8,128)}) custom-call(bf16[64,1024]{1,0:T(8,128)(2,1)} %bitcast.8, f32[32,1024]{1,0:T(8,128)} %bitcast.6, s32[2,4]{1,0:T(2,128)} %near_in.1, s32[1,128]{1,0:T(1,128)} %skeleton_in.1, s32[127,128]{1,0:T(8,128)} %upper_in.1, s32[2,16]{1,0:T(2,128)} %far_in.1), custom_call_target="tpu_custom_call" | custom-call | tf_op jit(solution)/shard_map/pallas_call | solution.py:396
  56.2 2.2 %shard_map.95 = (f32[32,1024]{1,0:T(8,128)}, f32[32,1024]{1,0:T(8,128)}, f32[32,1024]{1,0:T(8,128)}) custom-call(f32[32,128]{1,0:T(8,128)} %get-tuple-element.8.work, f32[32,1024]{1,0:T(8,128)} %bitcast.9, f32[32,1024]{1,0:T(8,128)} %bitcast.7, f32[32,1024]{1,0:T(8,128)} %get-tuple-element.9.image), custom_call_target="tpu_custom_call" | custom-call | tf_op jit(solution)/shard_map/pallas_call | solution.py:431

commit v6 on v5

--- a/solution.py
+++ b/solution.py
@@ -81,27 +81,14 @@
             src_ref=src, dst_ref=dst, send_sem=send, recv_sem=recv, device_id=device, device_id_type=MESH
         )
 
-    loads[0].wait()
-    row = lax.broadcasted_iota(jnp.int32, (16, 128), 0)
-    wanted = jnp.full((16, 128), -1, jnp.int32)
-    for leaf in range(2):
-        for n in range(NEAR):
-            wanted = jnp.where(row == leaf * NEAR + n, near[leaf, n], wanted)
-    asked[gy] = wanted.astype(F32).astype(BF16)
-    for load in loads[1:]:
+    for load in loads[1:4]:
         load.wait()
 
     @pl.loop(0, 2)
     def _(leaf):
         at = pl.ds(pl.multiple_of(leaf * LEAF, LEAF), LEAF)
-        wide = points[:, at].astype(F32)
-        rows = square_rows(wide)
         own_right[leaf, 0:D] = points[:, at]
-        own_right[leaf, D:AUG] = rows.astype(BF16)
-        both = jnp.concatenate([wide, turned(rows), jnp.zeros((48, LEAF), F32)], axis=0)
-        own_left[leaf] = both.T.astype(BF16)
-        own[leaf, 0:D] = points[:, at]
-        own[leaf, D:LEAF_ROWS] = residual[:, at].astype(BF16)
+        own_right[leaf, D:AUG] = square_rows(points[:, at].astype(F32)).astype(BF16)
 
     place = lax.broadcasted_iota(jnp.int32, (CPD, RANK), 0)
     skel = dot(points[...], jnp.where(place == skeleton[...], 1.0, 0.0).astype(BF16))
@@ -129,11 +116,31 @@
 
     @pl.loop(1, N_GY)
     def _(k):
+        pay_copy((gy + k) % N_GY, gy).start()
+
+    loads[0].wait()
+    row = lax.broadcasted_iota(jnp.int32, (16, 128), 0)
+    wanted = jnp.full((16, 128), -1, jnp.int32)
+    for leaf in range(2):
+        for n in range(NEAR):
+            wanted = jnp.where(row == leaf * NEAR + n, near[leaf, n], wanted)
+    asked[gy] = wanted.astype(F32).astype(BF16)
+
+    @pl.loop(1, N_GY)
+    def _(k):
         req_copy((gy + k) % N_GY, gy).start()
 
-    @pl.loop(1, N_GY)
-    def _(k):
-        pay_copy((gy + k) % N_GY, gy).start()
+    @pl.loop(0, 2)
+    def _(leaf):
+        at = pl.ds(pl.multiple_of(leaf * LEAF, LEAF), LEAF)
+        wide = own_right[leaf].astype(F32)
+        both = jnp.concatenate([wide[:D], turned(wide[D:]), jnp.zeros((48, LEAF), F32)], axis=0)
+        own_left[leaf] = both.T.astype(BF16)
+        own[leaf, 0:D] = points[:, at]
+        own[leaf, D:LEAF_ROWS] = residual[:, at].astype(BF16)
+
+    for load in loads[4:]:
+        load.wait()
 
     def tile_term(leaf, right, values):
         tile = jnp.exp2(SCALE * dot(own_left[leaf, :, :AUG], right)).astype(BF16)
@@ -360,19 +367,27 @@
         total += part2[k]
 
     work = jnp.concatenate([total, pltpu.roll(total, 64, 1)], axis=0)
-    row = lax.broadcasted_iota(jnp.int32, (NRHS, 128), 0)
 
     def eight(_, work):
-        for k in range(0, 8, 2):
-            first, second = (jnp.broadcast_to(work[:, k + i : k + i + 1], (NRHS, 128)) for i in range(2))
-            inverse = 1.0 / first[k : k + 1]
-            factor = first[k + 1 : k + 2] * inverse
-            below = 1.0 / (second[k + 1 : k + 2] - factor * second[k : k + 1])
-            lower = (work[k + 1 : k + 2] - factor * work[k : k + 1]) * below
-            upper_row = (work[k : k + 1] - second[k : k + 1] * lower) * inverse
-            rest = work - first * upper_row - second * lower
-            work = jnp.where(row == k, upper_row, jnp.where(row == k + 1, lower, rest))
-        return pltpu.roll(jnp.concatenate([work[8:], work[:8]], axis=0), 120, 1)
+        columns = [jnp.broadcast_to(work[:, i : i + 1], (NRHS, 128)) for i in range(8)]
+        block = [[columns[j][i : i + 1] for j in range(8)] for i in range(8)]
+        rows = [work[i : i + 1] for i in range(8)]
+        for i in range(8):
+            inverse = 1.0 / block[i][i]
+            rows[i] = rows[i] * inverse
+            for j in range(i + 1, 8):
+                block[i][j] = block[i][j] * inverse
+            for r in range(i + 1, 8):
+                for j in range(i + 1, 8):
+                    block[r][j] = block[r][j] - block[r][i] * block[i][j]
+                rows[r] = rows[r] - block[r][i] * rows[i]
+        for i in range(7, 0, -1):
+            for r in range(i):
+                rows[r] = rows[r] - block[r][i] * rows[i]
+        rest = work
+        for i in range(8):
+            rest = rest - columns[i] * rows[i]
+        return pltpu.roll(jnp.concatenate([rest[8:], *rows], axis=0), 120, 1)
 
     work = lax.fori_loop(0, NRHS // 8, eight, work)
     coeffs[...] = work

time: 58.5 us -> 56.9 us (0.973)
  Pallas kernels: 57.7 us -> 56.1 us
    pallas_call x1, Pallas kernels: 55.5 us -> 53.9 us  [shards(): pl.pallas_call(kernel_body, out_shape=(jax.ShapeDtypeStruct((NRHS, CPD),...]
where the time goes in v6:
time: 56.9 us; the launch traced here: 56.8 us
  Pallas kernels  56.1 us (99%)
  between operations  0.64 us (1%)
    pallas_call x1, Pallas kernels, shards(): pl.pallas_call(kernel_body, out_shape=(jax.ShapeDtypeStruct((NRHS, CPD),...  53.9 us
    pallas_call x1, Pallas kernels, shards(): pl.pallas_call(update_body, out_shape=(jax.ShapeDtypeStruct((NRHS, CPD),...  2.17 us

profile of v6, /device:TPU:1, one launch (start us, length us, event | category | flops | bytes accessed | tf_op | source)
XLA Modules:
  0.0 56.8 jit_solution(7513524510695593667)
XLA Ops:
  0.6 53.9 %shard_map.94 = (f32[32,1024]{1,0:T(8,128)}, f32[32,128]{1,0:T(8,128)}) custom-call(bf16[64,1024]{1,0:T(8,128)(2,1)} %bitcast.8, f32[32,1024]{1,0:T(8,128)} %bitcast.6, s32[2,4]{1,0:T(2,128)} %near_in.1, s32[1,128]{1,0:T(1,128)} %skeleton_in.1, s32[127,128]{1,0:T(8,128)} %upper_in.1, s32[2,16]{1,0:T(2,128)} %far_in.1), custom_call_target="tpu_custom_call" | custom-call | tf_op jit(solution)/shard_map/pallas_call | solution.py:411
  54.6 2.2 %shard_map.95 = (f32[32,1024]{1,0:T(8,128)}, f32[32,1024]{1,0:T(8,128)}, f32[32,1024]{1,0:T(8,128)}) custom-call(f32[32,128]{1,0:T(8,128)} %get-tuple-element.8.work, f32[32,1024]{1,0:T(8,128)} %bitcast.9, f32[32,1024]{1,0:T(8,128)} %bitcast.7, f32[32,1024]{1,0:T(8,128)} %get-tuple-element.9.image), custom_call_target="tpu_custom_call" | custom-call | tf_op jit(solution)/shard_map/pallas_call | solution.py:446

commit v7 on v6

--- a/solution.py
+++ b/solution.py
@@ -109,7 +109,11 @@
 
     def pay_copy(peer, slot):
         at = FIRST + gx * N_GY + slot
-        return copy(nodes.at[mine, pl.ds(0, SENT)], nodes.at[at, pl.ds(0, SENT)], pay_s.at[peer], pay_r.at[slot], (gx, peer))
+        return copy(nodes.at[mine, pl.ds(0, SENT)], nodes.at[at, pl.ds(0, SENT)], pay_s.at[0], pay_r.at[0], (gx, peer))
+
+    def all_pay():
+        part = nodes.at[pl.ds(FIRST + gx * N_GY, N_GY - 1), pl.ds(0, SENT)]
+        return copy(part, part, pay_s.at[0], pay_r.at[0], (gx, (gy + 1) % N_GY))
 
     def near_copy(peer, slot):
         return copy(stage.at[peer], leaves.at[slot], near_s.at[peer], near_r.at[slot], (gx, peer))
@@ -150,10 +154,7 @@
     def _(leaf):
         near_acc[leaf] = tile_term(leaf, own_right[leaf], own[leaf, D:LEAF_ROWS])
 
-    @pl.loop(1, N_GY)
-    def _(k):
-        peer = (gy + k) % N_GY
-        pay_copy(peer, peer).wait_recv()
+    all_pay().wait_recv()
 
     def half(row, h):
         return nodes.at[pl.ds(FIRST + row * N_GY + h * 8, 8), pl.ds(0, SENT)]
@@ -311,10 +312,18 @@
     part1[gy] = jnp.concatenate([gram[:16], gram[16:]], axis=1)
 
     def one_copy(peer, slot):
-        return copy(part1.at[gy], part1.at[slot], one_s.at[peer], one_r.at[slot], (gx, peer))
+        return copy(part1.at[gy], part1.at[slot], one_s.at[0], one_r.at[0], (gx, peer))
+
+    def all_one():
+        part = part1.at[pl.ds(0, N_GY - 1)]
+        return copy(part, part, one_s.at[0], one_r.at[0], (gx, (gy + 1) % N_GY))
+
+    def all_two():
+        part = part2.at[pl.ds(0, N_GX - 1)]
+        return copy(part, part, two_s.at[0], two_r.at[0], ((gx + 1) % N_GX, gy))
 
     def two_copy(peer, slot):
-        return copy(part2.at[gx], part2.at[slot], two_s.at[peer], two_r.at[slot], (peer, gy))
+        return copy(part2.at[gx], part2.at[slot], two_s.at[0], two_r.at[0], (peer, gy))
 
     @pl.loop(1, N_GY)
     def _(k):
@@ -324,9 +333,9 @@
     def _(k):
         peer = (gy + k) % N_GY
         req_copy(peer, gy).wait_send()
-        pay_copy(peer, gy).wait_send()
         near_copy(peer, gy).wait_send()
 
+    all_pay().wait_send()
     for step in (1, -1):
         for h in range(2):
             y_copy(step, h, 0).wait_send()
@@ -339,10 +348,7 @@
         for level in range(7, 2, -1):
             full_copy(i - 1, level, False).wait_send()
 
-    @pl.loop(1, N_GY)
-    def _(k):
-        peer = (gy + k) % N_GY
-        one_copy(peer, peer).wait_recv()
+    all_one().wait_recv()
 
     total = part1[0]
     for k in range(1, N_GY):
@@ -353,14 +359,9 @@
     def _(k):
         two_copy((gx + k) % N_GX, gx).start()
 
-    @pl.loop(1, N_GY)
-    def _(k):
-        one_copy((gy + k) % N_GY, gy).wait_send()
-
-    @pl.loop(1, N_GX)
-    def _(k):
-        peer = (gx + k) % N_GX
-        two_copy(peer, peer).wait_recv()
+    all_one().wait_send()
+
+    all_two().wait_recv()
 
     total = part2[0]
     for k in range(1, N_GX):
@@ -392,9 +393,7 @@
     work = lax.fori_loop(0, NRHS // 8, eight, work)
     coeffs[...] = work
 
-    @pl.loop(1, N_GX)
-    def _(k):
-        two_copy((gx + k) % N_GX, gx).wait_send()
+    all_two().wait_send()
 
 
 def update_body(work, solution, residual, image, solution_next, residual_next, image_out):
@@ -435,9 +434,9 @@
             pltpu.VMEM((N_GY, 16, 128), F32),
             pltpu.VMEM((N_GX, 16, 128), F32),
             dma((6,)),
-            dma((N_GY,)), dma((N_GY,)), dma((N_GY,)), dma((N_GY,)), dma((N_GY,)), dma((N_GY,)),
+            dma((N_GY,)), dma((N_GY,)), dma((1,)), dma((1,)), dma((N_GY,)), dma((N_GY,)),
             dma((2, 2)), dma((2, 2)), dma((2,)), dma((2,)), dma((2,)), dma((2,)), dma((N_Y, 5)), dma((N_Y, 5)),
-            dma((N_GY,)), dma((N_GY,)), dma((N_GX,)), dma((N_GX,)),
+            dma((1,)), dma((1,)), dma((1,)), dma((1,)),
         ],
         compiler_params=pltpu.CompilerParams(
             collective_id=0, has_side_effects=True, vmem_limit_bytes=60 * 2**20

time: 56.9 us -> 56 us (0.984)
  Pallas kernels: 56.1 us -> 55.3 us
    pallas_call x1, Pallas kernels: 53.9 us -> 53.1 us  [shards(): pl.pallas_call(kernel_body, out_shape=(jax.ShapeDtypeStruct((NRHS, CPD),...]
where the time goes in v7:
time: 56 us; the launch traced here: 55.9 us
  Pallas kernels  55.3 us (99%)
  between operations  0.64 us (1%)
    pallas_call x1, Pallas kernels, shards(): pl.pallas_call(kernel_body, out_shape=(jax.ShapeDtypeStruct((NRHS, CPD),...  53.1 us
    pallas_call x1, Pallas kernels, shards(): pl.pallas_call(update_body, out_shape=(jax.ShapeDtypeStruct((NRHS, CPD),...  2.17 us

profile of v7, /device:TPU:1, one launch (start us, length us, event | category | flops | bytes accessed | tf_op | source)
XLA Modules:
  0.0 55.9 jit_solution(242132123797510824)
XLA Ops:
  0.6 53.1 %shard_map.94 = (f32[32,1024]{1,0:T(8,128)}, f32[32,128]{1,0:T(8,128)}) custom-call(bf16[64,1024]{1,0:T(8,128)(2,1)} %bitcast.8, f32[32,1024]{1,0:T(8,128)} %bitcast.6, s32[2,4]{1,0:T(2,128)} %near_in.1, s32[1,128]{1,0:T(1,128)} %skeleton_in.1, s32[127,128]{1,0:T(8,128)} %upper_in.1, s32[2,16]{1,0:T(2,128)} %far_in.1), custom_call_target="tpu_custom_call" | custom-call | tf_op jit(solution)/shard_map/pallas_call | solution.py:410
  53.7 2.2 %shard_map.95 = (f32[32,1024]{1,0:T(8,128)}, f32[32,1024]{1,0:T(8,128)}, f32[32,1024]{1,0:T(8,128)}) custom-call(f32[32,128]{1,0:T(8,128)} %get-tuple-element.8.work, f32[32,1024]{1,0:T(8,128)} %bitcast.9, f32[32,1024]{1,0:T(8,128)} %bitcast.7, f32[32,1024]{1,0:T(8,128)} %get-tuple-element.9.image), custom_call_target="tpu_custom_call" | custom-call | tf_op jit(solution)/shard_map/pallas_call | solution.py:445

commit v8 on v7

--- a/solution.py
+++ b/solution.py
@@ -116,7 +116,11 @@
         return copy(part, part, pay_s.at[0], pay_r.at[0], (gx, (gy + 1) % N_GY))
 
     def near_copy(peer, slot):
-        return copy(stage.at[peer], leaves.at[slot], near_s.at[peer], near_r.at[slot], (gx, peer))
+        return copy(stage.at[peer], leaves.at[slot], near_s.at[0], near_r.at[0], (gx, peer))
+
+    def all_near():
+        src, dst = stage.at[pl.ds(0, N_GY - 1)], leaves.at[pl.ds(0, N_GY - 1)]
+        return copy(src, dst, near_s.at[0], near_r.at[0], (gx, (gy + 1) % N_GY))
 
     @pl.loop(1, N_GY)
     def _(k):
@@ -241,9 +245,12 @@
         return nodes.at[pl.ds(2**level - 1 + row * (2**level // N_GX), 2**level // N_GX)]
 
     def full_copy(step, level, other):
-        at = (y + step) % N_Y
-        send, recv = full_s.at[at, level - 3], full_r.at[at, level - 3]
-        return copy(run(row_of(step), level), run(row_of(step, other), level), send, recv, (sibling, gy))
+        src, dst = run(row_of(step), level), run(row_of(step, other), level)
+        return copy(src, dst, full_s.at[0], full_r.at[0], (sibling, gy))
+
+    def all_full():
+        part = nodes.at[pl.ds(0, 3 * (2 * N_GY - 1))]
+        return copy(part, part, full_s.at[0], full_r.at[0], (sibling, gy))
 
     @pl.loop(0, N_Y + 1)
     def _(i):
@@ -279,9 +286,7 @@
             for level in range(7, 2, -1):
                 full_copy(away, level, False).start()
 
-    for step in (0, 1, -1):
-        for level in range(7, 2, -1):
-            full_copy(step, level, True).wait_recv()
+    all_full().wait_recv()
 
     build(3, 4)
     build(1, 2)
@@ -295,10 +300,7 @@
         got = jnp.concatenate([nodes[far[leaf, 8 * group + i]] for i in range(8)], axis=1)
         far_acc[leaf] = far_acc[leaf] + tile_term(leaf, right_of(got), got[D:SENT])
 
-    @pl.loop(1, N_GY)
-    def _(k):
-        peer = (gy + k) % N_GY
-        near_copy(peer, peer).wait_recv()
+    all_near().wait_recv()
 
     pl.loop(0, NEAR)(near_tile)
 
@@ -333,9 +335,9 @@
     def _(k):
         peer = (gy + k) % N_GY
         req_copy(peer, gy).wait_send()
-        near_copy(peer, gy).wait_send()
 
     all_pay().wait_send()
+    all_near().wait_send()
     for step in (1, -1):
         for h in range(2):
             y_copy(step, h, 0).wait_send()
@@ -343,10 +345,7 @@
     for h in range(2):
         sib_copy(h, False).wait_send()
 
-    @pl.loop(0, 3)
-    def _(i):
-        for level in range(7, 2, -1):
-            full_copy(i - 1, level, False).wait_send()
+    all_full().wait_send()
 
     all_one().wait_recv()
 
@@ -434,8 +433,8 @@
             pltpu.VMEM((N_GY, 16, 128), F32),
             pltpu.VMEM((N_GX, 16, 128), F32),
             dma((6,)),
-            dma((N_GY,)), dma((N_GY,)), dma((1,)), dma((1,)), dma((N_GY,)), dma((N_GY,)),
-            dma((2, 2)), dma((2, 2)), dma((2,)), dma((2,)), dma((2,)), dma((2,)), dma((N_Y, 5)), dma((N_Y, 5)),
+            dma((N_GY,)), dma((N_GY,)), dma((1,)), dma((1,)), dma((1,)), dma((1,)),
+            dma((2, 2)), dma((2, 2)), dma((2,)), dma((2,)), dma((2,)), dma((2,)), dma((1,)), dma((1,)),
             dma((1,)), dma((1,)), dma((1,)), dma((1,)),
         ],
         compiler_params=pltpu.CompilerParams(

time: 56 us -> 55.4 us (0.989)
  Pallas kernels: 55.3 us -> 54.6 us
    pallas_call x1, Pallas kernels: 53.1 us -> 52.4 us  [shards(): pl.pallas_call(kernel_body, out_shape=(jax.ShapeDtypeStruct((NRHS, CPD),...]
where the time goes in v8:
time: 55.4 us; the launch traced here: 55.2 us
  Pallas kernels  54.6 us (99%)
  between operations  0.64 us (1%)
    pallas_call x1, Pallas kernels, shards(): pl.pallas_call(kernel_body, out_shape=(jax.ShapeDtypeStruct((NRHS, CPD),...  52.4 us
    pallas_call x1, Pallas kernels, shards(): pl.pallas_call(update_body, out_shape=(jax.ShapeDtypeStruct((NRHS, CPD),...  2.17 us

profile of v8, /device:TPU:1, one launch (start us, length us, event | category | flops | bytes accessed | tf_op | source)
XLA Modules:
  0.0 55.2 jit_solution(10746197864639962779)
XLA Ops:
  0.6 52.4 %shard_map.94 = (f32[32,1024]{1,0:T(8,128)}, f32[32,128]{1,0:T(8,128)}) custom-call(bf16[64,1024]{1,0:T(8,128)(2,1)} %bitcast.8, f32[32,1024]{1,0:T(8,128)} %bitcast.6, s32[2,4]{1,0:T(2,128)} %near_in.1, s32[1,128]{1,0:T(1,128)} %skeleton_in.1, s32[127,128]{1,0:T(8,128)} %upper_in.1, s32[2,16]{1,0:T(2,128)} %far_in.1), custom_call_target="tpu_custom_call" | custom-call | tf_op jit(solution)/shard_map/pallas_call | solution.py:409
  53.0 2.2 %shard_map.95 = (f32[32,1024]{1,0:T(8,128)}, f32[32,1024]{1,0:T(8,128)}, f32[32,1024]{1,0:T(8,128)}) custom-call(f32[32,128]{1,0:T(8,128)} %get-tuple-element.8.work, f32[32,1024]{1,0:T(8,128)} %bitcast.9, f32[32,1024]{1,0:T(8,128)} %bitcast.7, f32[32,1024]{1,0:T(8,128)} %get-tuple-element.9.image), custom_call_target="tpu_custom_call" | custom-call | tf_op jit(solution)/shard_map/pallas_call | solution.py:444

commit v9 on v8

--- a/solution.py
+++ b/solution.py
@@ -102,6 +102,7 @@
     nodes[mine, 0:D] = skel.astype(BF16)
     nodes[mine, D:SENT] = (weights * (1.0 / math.sqrt(CPD))).astype(BF16)
 
+    far_acc[...] = jnp.zeros_like(far_acc)
     pl.semaphore_wait(barrier, N_GY - 1 + N_GX - 1)
 
     def req_copy(peer, slot):
@@ -291,8 +292,6 @@
     build(3, 4)
     build(1, 2)
     build(0, 1)
-
-    far_acc[...] = jnp.zeros_like(far_acc)
 
     @pl.loop(0, FAR // 4)
     def _(n):

time: 55.4 us -> 55.4 us (level)
  no operation moved by 1% of the time
where the time goes in v9:
time: 55.4 us; the launch traced here: 55.2 us
  Pallas kernels  54.6 us (99%)
  between operations  0.64 us (1%)
    pallas_call x1, Pallas kernels, shards(): pl.pallas_call(kernel_body, out_shape=(jax.ShapeDtypeStruct((NRHS, CPD),...  52.4 us
    pallas_call x1, Pallas kernels, shards(): pl.pallas_call(update_body, out_shape=(jax.ShapeDtypeStruct((NRHS, CPD),...  2.17 us

profile of v9, /device:TPU:1, one launch (start us, length us, event | category | flops | bytes accessed | tf_op | source)
XLA Modules:
  0.0 55.2 jit_solution(16158703292219116963)
XLA Ops:
  0.6 52.4 %shard_map.94 = (f32[32,1024]{1,0:T(8,128)}, f32[32,128]{1,0:T(8,128)}) custom-call(bf16[64,1024]{1,0:T(8,128)(2,1)} %bitcast.8, f32[32,1024]{1,0:T(8,128)} %bitcast.6, s32[2,4]{1,0:T(2,128)} %near_in.1, s32[1,128]{1,0:T(1,128)} %skeleton_in.1, s32[127,128]{1,0:T(8,128)} %upper_in.1, s32[2,16]{1,0:T(2,128)} %far_in.1), custom_call_target="tpu_custom_call" | custom-call | tf_op jit(solution)/shard_map/pallas_call | solution.py:408
  53.0 2.2 %shard_map.95 = (f32[32,1024]{1,0:T(8,128)}, f32[32,1024]{1,0:T(8,128)}, f32[32,1024]{1,0:T(8,128)}) custom-call(f32[32,128]{1,0:T(8,128)} %get-tuple-element.8.work, f32[32,1024]{1,0:T(8,128)} %bitcast.9, f32[32,1024]{1,0:T(8,128)} %bitcast.7, f32[32,1024]{1,0:T(8,128)} %get-tuple-element.9.image), custom_call_target="tpu_custom_call" | custom-call | tf_op jit(solution)/shard_map/pallas_call | solution.py:443
